TPU v7x, 32 devices: a whole 2x2x4 slice. The times are simulated.
32 devices in a mesh: batch: 16 (over z, x, core), tp: 2 (over y).
Axes of the slice: x: 2, y: 2, z: 4, core: 2. Of those that a mesh axis runs over, the one named last changes fastest.
Arguments:
- inputs: bfloat16 [24576, 768], P(('batch', 'tp')), may hold values from -6 to 6
- cotangent: bfloat16 [24576, 768], P(('batch', 'tp')), may hold values from -6 to 6
- zinc_lengths: int32 [128], P(('batch', 'tp')), may hold values from 8 to 64, as said below
- pubchem_lengths: int32 [64], P(('batch', 'tp')), may hold values from 16 to 256, as said below
- feature_stack: float32 [8, 12, 32, 64], replicated, may hold values from -6 to 6
- train_step: int32 [1], replicated, may hold values from 0 to 999999
- redraw_interval: int32 [1], replicated, may hold values from 1 to 4999
- attn_gain: float32 [768], replicated, may hold values from 0.5 to 1.5
- attn_shift: float32 [768], replicated, may hold values from -1 to 1
- query_weight: bfloat16 [768, 768], replicated, may hold values from -0.21875 to 0.21875
- query_bias: float32 [768], replicated, may hold values from -1 to 1
- key_weight: bfloat16 [768, 768], replicated, may hold values from -0.21875 to 0.21875
- key_bias: float32 [768], replicated, may hold values from -1 to 1
- value_weight: bfloat16 [768, 768], replicated, may hold values from -0.21875 to 0.21875
- value_bias: float32 [768], replicated, may hold values from -1 to 1
- output_weight: bfloat16 [768, 768], replicated, may hold values from -0.625 to 0.625
- output_bias: float32 [768], replicated, may hold values from -1 to 1
- ffn_gain: float32 [768], replicated, may hold values from 0.5 to 1.5
- ffn_shift: float32 [768], replicated, may hold values from -1 to 1
- hidden_weight: bfloat16 [768, 3072], P(None, 'tp'), may hold values from -0.21875 to 0.21875
- hidden_bias: bfloat16 [3072], P('tp'), may hold values from -1 to 1
- return_weight: bfloat16 [3072, 768], P('tp'), may hold values from -0.109375 to 0.109375
- return_bias: float32 [768], replicated, may hold values from -1 to 1
Outputs:
- layer_out: bfloat16 [24576, 768], P(('batch', 'tp'))
- input_grad: bfloat16 [24576, 768], P(('batch', 'tp'))
- grad_attn_gain: float32 [768], replicated
- grad_attn_shift: float32 [768], replicated
- grad_query_weight: float32 [768, 768], replicated
- grad_query_bias: float32 [768], replicated
- grad_key_weight: float32 [768, 768], replicated
- grad_key_bias: float32 [768], replicated
- grad_value_weight: float32 [768, 768], replicated
- grad_value_bias: float32 [768], replicated
- grad_output_weight: float32 [768, 768], replicated
- grad_output_bias: float32 [768], replicated
- grad_ffn_gain: float32 [768], replicated
- grad_ffn_shift: float32 [768], replicated
- grad_hidden_weight: float32 [768, 3072], P(None, 'tp')
- grad_hidden_bias: float32 [3072], P('tp')
- grad_return_weight: float32 [3072, 768], P('tp')
- grad_return_bias: float32 [768], replicated
Inputs may be any that keep to these rules, and one draw needn't show every extreme that they name: `zinc_lengths`: each ZINC molecule has between 8 and 64 live slots. `pubchem_lengths`: each PubChem molecule has between 16 and 256 live slots.
All inputs are finite; a program needn't handle non-finite values.
Results may differ from a plain program's by a relative error of at most 0.018.
Values may be sent and summed in bfloat16 or wider, within the bound.
No kernel may reach another device: no remote copies, remote signals or barrier semaphores. Data moves between devices by JAX's collectives and lax.ppermute only.
A program may use at most 256 MiB of HBM per device.

v0:
```python
import functools
import math

import jax
import jax.numpy as jnp
import numpy as np
from jax import lax
from jax.experimental import pallas as pl
from jax.experimental.pallas import tpu as pltpu
from jax.sharding import PartitionSpec as P

ZPAD = 64
PPAD = 256
F32 = jnp.float32
BF = jnp.bfloat16
VM = pltpu.VMEM
GROUP = 4
S = jax.ShapeDtypeStruct
TIMES = {"attend_fwd": 24, "ffn_chunk": 17, "layer_end": 9, "mid": 8, "value_bwd": 13, "query_bwd": 13, "input_back": 10, "finish_ffn": 5, "finish_pair": 5}
MIB = 2**20
GRANT = 52


def dot(a, b):
    return jnp.dot(a, b, preferred_element_type=F32)


def dot_t(a, b):
    return lax.dot_general(a, b, (((1,), (1,)), ((), ())), preferred_element_type=F32)


def dot_c(a, b):
    return lax.dot_general(a, b, (((0,), (0,)), ((), ())), preferred_element_type=F32)


def split(v):
    hi = v.astype(BF)
    return hi, (v - hi.astype(F32)).astype(BF)


def norm_parts(values):
    center = values - jnp.mean(values, axis=-1, keepdims=True)
    rate = lax.rsqrt(jnp.mean(center * center, axis=-1, keepdims=True) + 1e-05)
    return center * rate, rate


def row(ref):
    return ref[...].reshape(1, -1)


def block_mask(width):
    f = lax.broadcasted_iota(jnp.int32, (128, width), 0) // 32
    c = lax.broadcasted_iota(jnp.int32, (128, width), 1) % 256 // 64
    return f == c


def molecules(zm, pm):
    return [(i * ZPAD, ZPAD) for i in range(zm)] + [(zm * ZPAD + i * PPAD, PPAD) for i in range(pm)]


def members(mols, b):
    return [(i, r, n) for i, (r, n) in enumerate(mols) if b * PPAD <= r < (b + 1) * PPAD]


class Mover:
    def __init__(self, sems):
        self.sems, self.n, self.out = sems, 0, []

    def load(self, src, dst):
        copy = pltpu.make_async_copy(src, dst, self.sems.at[self.n])
        self.n += 1
        copy.start()
        return copy

    def store(self, src, dst):
        self.out.append(self.load(src, dst))

    def finish(self):
        for copy in self.out:
            copy.wait()


def call(kernel, name, args, spaces, outs, scratch, copies, flops, moved, aliases=None, after=()):
    n, extra = len(args), len(after)

    def body(*refs):
        kernel(*refs[:n], *refs[n + extra:])

    spec = {
        "v": pl.BlockSpec(memory_space=VM),
        "h": pl.BlockSpec(memory_space=pltpu.HBM),
        "s": pl.BlockSpec(memory_space=pltpu.SMEM),
    }
    return pl.pallas_call(
        body,
        out_shape=tuple(o for _, o in outs),
        in_specs=[spec[s] for s in spaces] + [spec["h"]] * extra,
        out_specs=tuple(spec[s] for s, _ in outs),
        scratch_shapes=list(scratch) + [pltpu.SemaphoreType.DMA((copies,))],
        input_output_aliases=aliases or {},
        compiler_params=pltpu.CompilerParams(vmem_limit_bytes=GRANT * MIB),
        cost_estimate=pl.CostEstimate(flops=int(TIMES[name] * 1.15e9), bytes_accessed=moved, transcendentals=0),
        name=name,
    )(*args, *after)


def place_heads(scaled):
    two = jnp.concatenate([scaled, scaled], axis=1)
    return jnp.where(block_mask(256), jnp.concatenate([two, two], axis=1), 0.0)


def attend_fwd_kernel(zm, pm, meta, zlen, plen, cot_h, x_h, gain_h, shift_h, bq_h, bk_h, bv_h, bo_h, gain2_h, shift2_h,
                      wq_h, wk_h, wv_h, wo_h, stack_h, table_h, energy_h,
                      qkv_h, f_h, state_h, trans_h, middle_h, n2_h, left_h, proj_h,
                      cot, n2_s, left, x, vec, wq, wk, wv, wo, fp, proj, table, energy, qkv, f_s, state_s, trans, middle_s, att_s, sems):
    move = Mover(sems)
    rows, d = x.shape
    first = [move.load(x_h, x), move.load(gain_h, vec.at[0]), move.load(shift_h, vec.at[1]), move.load(stack_h.at[meta[5]], fp),
             move.load(cot_h, cot)]
    later = [move.load(s, t) for s, t in ((wq_h, wq), (bq_h, vec.at[2]), (table_h, table), (energy_h, energy), (wk_h, wk),
                                          (bk_h, vec.at[3]), (wv_h, wv), (bv_h, vec.at[4]))]
    last = [move.load(s, t) for s, t in ((wo_h, wo), (bo_h, vec.at[5]), (gain2_h, vec.at[6]), (shift2_h, vec.at[7]))]
    mols = molecules(zm, pm)
    groups = d // 256
    blocks = range(rows // PPAD)
    keep = block_mask(512)
    ones = jnp.ones((PPAD, 256), BF)

    def vector(i):
        return vec[i].reshape(1, -1)

    for c in first:
        c.wait()
    for g in range(groups):
        p = fp[g * GROUP:(g + 1) * GROUP].reshape(GROUP * 32, 64) * 64 ** -0.25
        turned = jnp.concatenate([p[:, 32:], -p[:, :32]], axis=1)
        hi, lo = split(jnp.concatenate([place_heads(p), place_heads(turned)], axis=1))
        proj[0, g] = hi
        proj[1, g] = lo
    n1s = {}
    for b in blocks:
        rs = slice(b * PPAD, (b + 1) * PPAD)
        normed, _ = norm_parts(x[rs, :].astype(F32))
        n1s[b] = (normed * vector(0) + vector(1)).astype(BF)
        trans[1, :, rs] = n1s[b].T
        left[1, :, rs] = cot[rs, :].T
    for c in later:
        c.wait()
    move.store(proj.at[0], proj_h)
    move.store(trans.at[1], trans_h.at[1])
    move.store(left.at[1], left_h.at[1])
    for b in blocks:
        mem = members(mols, b)
        rs = slice(b * PPAD, (b + 1) * PPAD)
        n1 = n1s[b]
        cosb, sinb = (jnp.concatenate([table[t, :n, :] for _, _, n in mem], axis=0) for t in range(2))
        cosb = jnp.concatenate([cosb, cosb], axis=1)
        sinb = jnp.concatenate([sinb, sinb], axis=1)
        live = jnp.concatenate(
            [(lax.broadcasted_iota(jnp.int32, (n, 128), 0) < (zlen[i] if i < zm else plen[i - zm])).astype(F32) for i, r, n in mem], axis=0)
        for g in range(groups):
            cs = slice(g * 256, (g + 1) * 256)
            fs = slice(g * 128, (g + 1) * 128)

            def features(w, bias, slot):
                v = dot(n1, w[:, cs]) + vector(bias)[:, cs]
                qkv[slot, rs, cs] = v.astype(BF)
                ch, cl = split(v * cosb)
                sh, sl = split(v * sinb)
                eh, el = split(v * v)
                ph, plo = proj[0, g], proj[1, g]
                e = energy[...]
                inner = (dot_t(ch, ph[:, :256]) + dot_t(sh, ph[:, 256:]) + dot_t(cl, ph[:, :256]) + dot_t(sl, ph[:, 256:])
                         + dot_t(ch, plo[:, :256]) + dot_t(sh, plo[:, 256:]) - dot_t(eh, e) - dot_t(el, e))
                return jnp.exp(inner) * (32 ** -0.5)

            fq = features(wq, 2, 0).astype(BF)
            fk = (features(wk, 3, 1) * live).astype(BF)
            f_s[0, rs, fs] = fq
            f_s[1, rs, fs] = fk
            v = (dot(n1, wv[:, cs]) + vector(4)[:, cs]).astype(BF)
            qkv[2, rs, cs] = v
            for i, r, n in mem:
                ms = slice(r - b * PPAD, r - b * PPAD + n)
                vo = jnp.concatenate([v[ms], ones[:n]], axis=1)
                state = jnp.where(keep, dot_c(fk[ms], vo), 0.0).astype(BF)
                state_s[i, g] = state
                nd = dot(fq[ms], state)
                att_s[r:r + n, cs] = (nd[:, :256] / nd[:, 256:]).astype(BF)
    for s, t in ((qkv, qkv_h), (f_s, f_h), (state_s, state_h)):
        move.store(s, t)
    for c in last:
        c.wait()
    for b in blocks:
        rs = slice(b * PPAD, (b + 1) * PPAD)
        trans[0, :, rs] = att_s[rs, :].T
        middle = x[rs, :].astype(F32) + (dot(att_s[rs, :], wo[...]) + vector(5))
        middle_s[rs, :] = middle
        normed, _ = norm_parts(middle)
        n2 = (normed * vector(6) + vector(7)).astype(BF)
        n2_s[rs, :] = n2
        left[0, :, rs] = n2.T
    move.store(middle_s, middle_h)
    move.store(n2_s, n2_h)
    move.store(trans.at[0], trans_h.at[0])
    move.store(left.at[0], left_h.at[0])
    move.finish()


def rotary_const():
    place = np.arange(PPAD, dtype=np.float64)
    rates = np.exp(np.arange(32, dtype=np.float64) * (-2.0 * math.log(10000.0) / 64))
    ang = place[:, None] * rates[None, :]
    return np.tile(np.stack([np.cos(ang), np.sin(ang)]), (1, 1, 4)).astype(np.float32)


def head_const(scale):
    f = np.arange(128)[:, None] // 32
    c = np.arange(256)[None, :] // 64
    return ((f == c) * scale).astype(jnp.bfloat16)


def attend_fwd(meta, zlen, plen, cot, x, vectors, wq, wk, wv, wo, stack, table):
    rows, d = x.shape
    zm, pm = zlen.shape[0], plen.shape[0]
    groups = d // 256
    states = (zm + pm, groups, 128, 512)
    outs = [S((3, rows, d), BF), S((2, rows, d // 2), BF), S(states, BF), S((2, d, rows), BF),
            S((rows, d), F32), S((rows, d), BF), S((2, d, rows), BF), S((groups, 128, 512), BF)]
    args = (meta, zlen, plen, cot, x, *vectors, wq, wk, wv, wo, stack, table, head_const(1 / 16))
    scratch = ([VM((rows, d), BF)] * 2 + [VM((2, d, rows), BF), VM((rows, d), BF), VM((8, d), F32)] + [VM((d, d), BF)] * 4
               + [VM(stack.shape[1:], F32), VM((2, groups, 128, 512), BF), VM(table.shape, F32), VM((128, 256), BF)]
               + [VM((3, rows, d), BF), VM((2, rows, d // 2), BF), VM(states, BF), VM((2, d, rows), BF), VM((rows, d), F32), VM((rows, d), BF)])
    return call(
        functools.partial(attend_fwd_kernel, zm, pm), "attend_fwd", args, "sss" + "h" * (len(args) - 3),
        [("h", o) for o in outs], scratch, 32, 2 * rows * d * d * 4, 16 * MIB)


def gelu_parts(h):
    bell = jnp.exp(h * h * -0.5)
    t = 1.0 / (1.0 + (0.3275911 * math.sqrt(0.5)) * jnp.abs(h))
    poly = t * (0.127414796 + t * (-0.142248368 + t * (0.7107068705 + t * (-0.7265760135 + t * 0.5307027145))))
    tail = poly * bell
    phi = jnp.where(h >= 0, 1.0 - tail, tail)
    return h * phi, phi + h * bell * (1.0 / math.sqrt(2 * math.pi))


def place_pieces(code, src, dst):
    n, step = src.shape[0], src.shape[1]
    for p in range(n):
        off = pl.multiple_of(jnp.bitwise_xor(p, code) * step, 16)
        dst[pl.ds(off, step), :] = src[p]


def ffn_kernel(pieces, shards, k, per, meta, n2_h, left_h, cot_h, hb_h, hw_h, rw_h, *refs):
    parts = {j: refs[(j - 1) * per:j * per] for j in range(1, shards)}
    hbs = refs[(shards - 1) * per:(shards - 1) * (per + 1)]
    e_prev = refs[(shards - 1) * (per + 1)] if k else None
    (gone_h, stay_h, keep_h, act_h, bias_o, e_h, rws_h, n2, left, cot, hb, hw, rw, hw2, rw2, right, stage, e_s, sems) = refs[-19:]
    move = Mover(sems)
    d, width = hw.shape[1:]
    half_d = d // 2
    me, code = meta[0], meta[1]
    order = list(range(1, shards)) + [0]
    early, late = {}, {}
    for j in order:
        early[j] = [move.load(hbs[j - 1] if j else hb_h, hb.at[j])]
        if j == order[0]:
            early[j].append(move.load(n2_h, n2))
        late[j] = []
        if j == 0:
            early[j].append(move.load(hw_h.at[:, k * width:(k + 1) * width], hw.at[0]))
            late[j].append(move.load(rw_h.at[k * width:(k + 1) * width, :], rw.at[0]))
        elif per == 2:
            early[j] += [move.load(parts[j][p].at[:half_d], hw2.at[j - 1, p]) for p in range(2)]
            late[j] += [move.load(parts[j][p].at[half_d:], rw2.at[j - 1, p]) for p in range(2)]
        else:
            early[j] += [move.load(parts[j][p], hw2.at[j - 1, p]) for p in range(2)]
            late[j] += [move.load(parts[j][2 + p], rw2.at[j - 1, p]) for p in range(2)]
        if j == order[0]:
            late[j].append(move.load(cot_h, cot))
    last = [move.load(left_h, left)]
    if k:
        last.append(move.load(e_prev, e_s))
    step, half = d // pieces, pieces // 2
    tile = width
    for j in order:
        for c in early[j] + late[j]:
            c.wait()
        if j:
            place_pieces(me, hw2.at[j - 1], hw.at[j])
            place_pieces(me, rw2.at[j - 1], rw.at[j])
        bias = hb[j].reshape(1, -1)[:, k * width:(k + 1) * width].astype(F32)
        for c in range(0, width, tile):
            cs = slice(c, c + tile)
            h = dot(n2[...], hw[j, :, cs]) + bias[:, cs]
            act, slope = gelu_parts(h)
            ga = dot_t(cot[...], rw[j, cs, :])
            gh = (ga * slope).astype(BF)
            right[0, j, :, cs] = gh
            right[1, j, :, cs] = act.astype(BF)
            bias_o[j:j + 1, cs] = jnp.sum(gh.astype(F32), axis=0, keepdims=True)
        move.store(right.at[1, j], act_h.at[j])
        move.store(rw.at[j], rws_h.at[j])
    for c in last:
        c.wait()
    for c in range(0, d, 768):
        cs = slice(c, c + 768)
        part = sum(dot_t(right[0, j], hw[j, cs, :]) for j in order)
        e_s[:, cs] = e_s[:, cs] + part if k else part
    move.store(e_s, e_h)
    for kind, slot in ((1 - me, 0), (me, 1)):
        for j in order:
            for c in range(0, width, tile):
                cs = slice(c, c + tile)
                value = dot(left[kind], right[kind, j, :, cs]).astype(BF)
                for p in range(pieces):
                    rel = jnp.bitwise_xor(p, code)
                    second = rel // half * (shards * half) + j * half + rel % half
                    off = pl.multiple_of(jnp.where(kind == 0, j * pieces + rel, second) * step, 16)
                    stage[slot, pl.ds(off, step), cs] = value[p * step:(p + 1) * step]
        if slot:
            move.store(stage.at[1], keep_h)
        else:
            cut = shards * d // 2
            move.store(stage.at[0, cut:], gone_h)
            move.store(stage.at[0, :cut], stay_h)
    move.finish()


def ffn_chunk(meta, pieces, shards, n2, left, cot, hb, hw, rw, parts, hbs, k, width, before, after=()):
    rows, d = n2.shape
    per = len(parts[0])
    part = S((shards * d // 2, width), BF)
    outs = [("h", part), ("h", part), ("h", S((shards * d, width), BF)), ("h", S((shards, rows, width), BF)), ("v", S((shards, width), F32)),
            ("h", S((rows, d), F32)), ("h", S((shards, width, d), BF))]
    scratch = [VM((rows, d), BF), VM((2, d, rows), BF), VM((rows, d), BF), VM((shards, 1) + hb.shape, BF), VM((shards, d, width), BF),
               VM((shards, width, d), BF), VM((shards - 1, 2, d // 2, width), BF), VM((shards - 1, 2, width // 2, d), BF),
               VM((2, shards, rows, width), BF), VM((2, shards * d, width), BF), VM((rows, d), F32)]
    args = (meta, n2, left, cot, hb.reshape(1, -1), hw, rw) + tuple(p for part in parts for p in part) + tuple(b.reshape(1, -1) for b in hbs) + tuple(before)
    return call(
        functools.partial(ffn_kernel, pieces, shards, k, per), "ffn_chunk", args,
        "s" + "h" * (len(args) - 1), outs, scratch, 12 + 13 * shards, 2 * rows * d * width * 5 * shards, 12 * MIB, None, after)


def products(move, pieces, codes, stage, outs):
    for slot, (left, right, out) in enumerate(outs):
        d = out.shape[0]
        step = d // pieces
        for c in range(0, d, 768):
            cs = slice(c, c + 768)
            value = dot(left[...], right[:, cs]).astype(BF)
            for p in range(pieces):
                off = pl.multiple_of(jnp.bitwise_xor(p, codes[slot]) * step, 16)
                stage[slot, pl.ds(off, step), cs] = value[p * step:(p + 1) * step]
        move.store(stage.at[slot], out)


def mid_kernel(e_h, cot_h, middle_h, wo_h, vec_h, gm_h, gb_h, gatt_h, vec_o, e_s, cot, middle, wo, vec, gm_s, gb_s, gatt, sems):
    move = Mover(sems)
    rows, d = middle.shape
    loads = [[move.load(s.at[r:r + 256], t.at[r:r + 256]) for s, t in ((middle_h, middle), (e_h, e_s), (cot_h, cot))]
             for r in range(0, rows, 256)]
    gain = move.load(vec_h, vec)
    last = move.load(wo_h, wo)
    gain.wait()
    gain2 = row(vec)
    acc_g = acc_s = acc_b = acc_c = 0.0
    for i, r in enumerate(range(0, rows, 256)):
        for c in loads[i]:
            c.wait()
        rs = slice(r, r + 256)
        e = e_s[rs, :]
        n, rate = norm_parts(middle[rs, :])
        c = cot[rs, :].astype(F32)
        acc_g += jnp.sum(e * n, axis=0, keepdims=True)
        acc_s += jnp.sum(e, axis=0, keepdims=True)
        acc_c += jnp.sum(c, axis=0, keepdims=True)
        eg = e * gain2
        gm = c + rate * (eg - jnp.mean(eg, axis=-1, keepdims=True) - n * jnp.mean(eg * n, axis=-1, keepdims=True))
        gm_s[rs, :] = gm
        gb = gm.astype(BF)
        gb_s[rs, :] = gb
        acc_b += jnp.sum(gb.astype(F32), axis=0, keepdims=True)
    for i, acc in enumerate((acc_g, acc_s, acc_b, acc_c)):
        vec_o[i:i + 1, :] = acc
    move.store(gm_s, gm_h)
    move.store(gb_s, gb_h)
    last.wait()
    for c in range(0, d, 768):
        cs = slice(c, c + 768)
        gatt[:, cs] = dot_t(gb_s[...], wo[cs, :]).astype(BF)
    move.store(gatt, gatt_h)
    move.finish()


def mid(e, cot, middle, wo, gain2, after=()):
    rows, d = middle.shape
    outs = [("h", S((rows, d), F32)), ("h", S((rows, d), BF)), ("h", S((rows, d), BF)), ("v", S((4, d), F32))]
    scratch = [VM((rows, d), F32), VM((rows, d), BF), VM((rows, d), F32), VM((d, d), BF), VM(gain2.shape, F32), VM((rows, d), F32),
               VM((rows, d), BF), VM((rows, d), BF)]
    args = (e, cot, middle, wo, gain2)
    return call(mid_kernel, "mid", args, "h" * len(args), outs, scratch, 8 + 3 * (rows // 256), 2 * rows * d * d, 8 * MIB, None, after)


def value_bwd_kernel(zm, pm, pieces, meta, gatt_h, gb_h, f_h, state_h, trans_h,
                     send_h, keep_h, gv_h, uw_h, gst_h, vec_o, gatt, uw_o, gst_o, f, state, left, right, stage, sems):
    move = Mover(sems)
    mols = molecules(zm, pm)
    rows, d = gatt.shape
    groups = d // 256
    loads = []
    for g in range(groups):
        cs, fs = slice(g * 256, (g + 1) * 256), slice(g * 128, (g + 1) * 128)
        loads.append([move.load(f_h.at[:, :, fs], f.at[:, :, fs]), move.load(state_h.at[:, g], state.at[:, g]),
                      move.load(gatt_h.at[:, cs], gatt.at[:, cs])])
    last = [move.load(trans_h, left), move.load(gb_h, right.at[0])]
    keep = block_mask(512)
    for g in range(groups):
        for c in loads[g]:
            c.wait()
        cs = slice(g * 256, (g + 1) * 256)
        fs = slice(g * 128, (g + 1) * 128)
        total = 0.0
        for i, (r, n) in enumerate(mols):
            ms = slice(r, r + n)
            st = state[i, g]
            q = f[0, ms, fs]
            nd = dot(q, st)
            rden = 1.0 / nd[:, 256:]
            u = gatt[ms, cs].astype(F32) * rden
            uw = jnp.concatenate([u, -(u * (nd[:, :256] * rden))], axis=1).astype(BF)
            uw_o[ms, slice(g * 512, (g + 1) * 512)] = uw
            gst = jnp.where(keep, dot_c(q, uw), 0.0).astype(BF)
            gst_o[i, g] = gst
            gv = dot(f[1, ms, fs], gst[:, :256]).astype(BF)
            right[1, ms, cs] = gv
            total += jnp.sum(gv.astype(F32), axis=0, keepdims=True)
        vec_o[0:1, cs] = total
    move.store(right.at[1], gv_h)
    move.store(uw_o, uw_h)
    move.store(gst_o, gst_h)
    for c in last:
        c.wait()
    me = meta[0]
    products(move, pieces, (meta[3], meta[2]), stage, ((left.at[1 - me], right.at[1 - me], send_h), (left.at[me], right.at[me], keep_h)))
    move.finish()


def value_bwd(meta, zm, pm, pieces, gatt, gb, f, state, trans, after=()):
    rows, d = gatt.shape
    outs = [("h", S((d, d), BF))] * 2 + [("h", S((rows, d), BF)), ("h", S((rows, 2 * d), BF)), ("h", S(state.shape, BF)), ("v", S((1, d), F32))]
    scratch = [VM((rows, d), BF), VM((rows, 2 * d), BF), VM(state.shape, BF), VM(f.shape, BF), VM(state.shape, BF), VM((2, d, rows), BF),
               VM((2, rows, d), BF), VM((2, d, d), BF)]
    args = (meta, gatt, gb, f, state, trans)
    return call(functools.partial(value_bwd_kernel, zm, pm, pieces), "value_bwd", args, "shhhhh", outs, scratch,
                10 + 3 * d // 256, 2 * d**3 * 3, 8 * MIB, None, after)


def query_bwd_kernel(zm, pm, pieces, meta, uw_h, gst_h, qkv_h, f_h, state_h, trans_h, proj_h, energy_h, table_h,
                     send_h, keep_h, gqk_h, vec_o, uw, gst, qkv, f, state, n1t, proj, energy, table, gqk, stage, sems):
    move = Mover(sems)
    mols = molecules(zm, pm)
    _, rows, d = qkv.shape
    loads = [[move.load(s, t) for s, t in ((proj_h, proj), (energy_h, energy), (table_h, table))]]
    for g in range(d // 256):
        cs, fs, us = slice(g * 256, (g + 1) * 256), slice(g * 128, (g + 1) * 128), slice(g * 512, (g + 1) * 512)
        if g:
            loads.append([])
        loads[g] += [move.load(uw_h.at[:, us], uw.at[:, us]), move.load(state_h.at[:, g], state.at[:, g]),
                     move.load(f_h.at[:, :, fs], f.at[:, :, fs]), move.load(gst_h.at[:, g], gst.at[:, g]),
                     move.load(qkv_h.at[:, :, cs], qkv.at[:, :, cs])]
    later = [move.load(trans_h.at[1], n1t)]
    for g in range(d // 256):
        for c in loads[g]:
            c.wait()
        cs = slice(g * 256, (g + 1) * 256)
        fs = slice(g * 128, (g + 1) * 128)
        sums = [0.0, 0.0]
        for b in range(rows // PPAD):
            mem = members(mols, b)
            rs = slice(b * PPAD, (b + 1) * PPAD)
            gfq, gfk = [], []
            for i, r, n in mem:
                ms = slice(r, r + n)
                gfq.append(dot_t(uw[ms, slice(g * 512, (g + 1) * 512)], state[i, g]))
                gfk.append(dot_t(jnp.concatenate([qkv[2, ms, cs], jnp.ones((n, 256), BF)], axis=1), gst[i, g]))
            cosb, sinb = (jnp.concatenate([table[t, :n, :] for _, _, n in mem], axis=0) for t in range(2))
            cosb = jnp.concatenate([cosb, cosb], axis=1)
            sinb = jnp.concatenate([sinb, sinb], axis=1)
            for t, gf in enumerate((gfq, gfk)):
                gp = (jnp.concatenate(gf, axis=0) * f[t, rs, fs].astype(F32)).astype(BF)
                back = dot(gp, proj[g])
                tot = dot(gp, energy[...])
                grad = (cosb * back[:, :256] + sinb * back[:, 256:] - tot * qkv[t, rs, cs].astype(F32)).astype(BF)
                gqk[t, rs, cs] = grad
                sums[t] += jnp.sum(grad.astype(F32), axis=0, keepdims=True)
        for t in range(2):
            vec_o[t:t + 1, cs] = sums[t]
    for c in later:
        c.wait()
    me = meta[0]
    products(move, pieces, (meta[3], meta[2]), stage, ((n1t, gqk.at[1 - me], send_h), (n1t, gqk.at[me], keep_h)))
    move.store(gqk, gqk_h)
    move.finish()


def query_bwd(meta, zm, pm, pieces, uw, gst, qkv, f, state, trans, proj, table, after=()):
    _, rows, d = qkv.shape
    outs = [("h", S((d, d), BF))] * 2 + [("h", S((2, rows, d), BF)), ("v", S((2, d), F32))]
    scratch = [VM(uw.shape, BF), VM(gst.shape, BF), VM(qkv.shape, BF), VM(f.shape, BF), VM(state.shape, BF), VM((d, rows), BF),
               VM(proj.shape, BF), VM((128, 256), BF), VM(table.shape, F32), VM((2, rows, d), BF), VM((2, d, d), BF)]
    args = (meta, uw, gst, qkv, f, state, trans, proj, head_const(64 ** -0.5), table)
    return call(functools.partial(query_bwd_kernel, zm, pm, pieces), "query_bwd", args, "s" + "h" * (len(args) - 1), outs, scratch,
                8 + 5 * d // 256, 2 * d**3 * 6, 12 * MIB, None, after)


def input_kernel(gqk_h, gv_h, wq_h, wk_h, wv_h, x_h, gm_h, gain_h, out_h, vec_o, gqk, gv, wq, wk, wv, x, gm, vec, e_s, out_s, sems):
    move = Mover(sems)
    rows, d = x.shape
    loads = [(move.load(gqk_h.at[0], gqk.at[0]), move.load(wq_h, wq)), (move.load(gqk_h.at[1], gqk.at[1]), move.load(wk_h, wk)),
             (move.load(gv_h, gv), move.load(wv_h, wv))]
    last = [move.load(s, t) for s, t in ((x_h, x), (gm_h, gm), (gain_h, vec))]
    for (left, right), load in zip(((gqk.at[0], wq), (gqk.at[1], wk), (gv, wv)), loads):
        for c in load:
            c.wait()
        for c in range(0, d, 768):
            cs = slice(c, c + 768)
            part = dot_t(left[...], right[cs, :])
            e_s[:, cs] = part if right is wq else e_s[:, cs] + part
    for c in last:
        c.wait()
    gain = row(vec)
    acc_g = acc_s = 0.0
    for r in range(0, rows, 256):
        rs = slice(r, r + 256)
        e = e_s[rs, :]
        n, rate = norm_parts(x[rs, :].astype(F32))
        acc_g += jnp.sum(e * n, axis=0, keepdims=True)
        acc_s += jnp.sum(e, axis=0, keepdims=True)
        eg = e * gain
        gx = rate * (eg - jnp.mean(eg, axis=-1, keepdims=True) - n * jnp.mean(eg * n, axis=-1, keepdims=True))
        out_s[rs, :] = (gm[rs, :] + gx).astype(BF)
    move.store(out_s, out_h)
    vec_o[0:1, :] = acc_g
    vec_o[1:2, :] = acc_s
    move.finish()


def input_back(gqk, gv, wq, wk, wv, x, gm, gain, after=()):
    rows, d = x.shape
    scratch = [VM(gqk.shape, BF), VM(gv.shape, BF)] + [VM((d, d), BF)] * 3 + [
        VM((rows, d), BF), VM((rows, d), F32), VM(gain.shape, F32), VM((rows, d), F32), VM((rows, d), BF)]
    args = (gqk, gv, wq, wk, wv, x, gm, gain)
    return call(input_kernel, "input_back", args, "h" * len(args), [("h", S((rows, d), BF)), ("v", S((2, d), F32))], scratch,
                16, 2 * d**3 * 3, 8 * MIB, None, after)


def layer_kernel(chunks, middle_h, vec_h, *refs):
    rights_h, rws_h = refs[:chunks], refs[chunks:2 * chunks]
    out_h, acts, rws, middle, vec, out_s, sems = refs[2 * chunks:]
    move = Mover(sems)
    base = [move.load(middle_h, middle), move.load(vec_h, vec)]
    loads = [[move.load(rights_h[k], acts.at[k]), move.load(rws_h[k], rws.at[k])] for k in range(chunks)]
    d = middle.shape[1]
    for c in base:
        c.wait()
    for k, load in enumerate(loads):
        for c in load:
            c.wait()
        for c in range(0, d, 768):
            cs = slice(c, c + 768)
            total = middle[:, cs] + sum(dot(acts[k, j], rws[k, j, :, cs]) for j in range(acts.shape[1]))
            if k + 1 < chunks:
                middle[:, cs] = total
            else:
                out_s[:, cs] = (total + row(vec)[:, cs]).astype(BF)
    move.store(out_s, out_h)
    move.finish()


def layer_end(rights, rws, middle, vec, after=()):
    rows, d = middle.shape
    k = len(rights)
    shards, _, width = rights[0].shape
    scratch = [VM((k, shards, rows, width), BF), VM((k, shards, width, d), BF), VM((rows, d), F32), VM(vec.shape, F32), VM((rows, d), BF)]
    args = (middle, vec, *rights, *rws)
    return call(functools.partial(layer_kernel, k), "layer_end", args, "h" * len(args),
                [("h", S((rows, d), BF))], scratch, 4 + 2 * k, 2 * rows * d * k * shards * width, 12 * MIB, None, after)[0]


def placed(ref, p, code, pieces):
    step = ref.shape[0] // pieces
    return ref[pl.ds(pl.multiple_of(jnp.bitwise_xor(p, code) * step, 16), step), :]


def load_halves(move, m0, m1, t0, t1, cols, both, me):
    half = m0.shape[0]
    return [move.load(m0.at[:, cols], both.at[me, :half]), move.load(m1.at[:, cols], both.at[me, half:]),
            move.load(t0.at[:, cols], both.at[1 - me, :half]), move.load(t1.at[:, cols], both.at[1 - me, half:])]


def finish_ffn_kernel(pieces, k, meta, m0, m1, t0, t1, *refs):
    ghw_h, grw_h, both, whole, wide, tall, sems = refs[-7:]
    move = Mover(sems)
    me, code = meta[0], meta[1]
    d, width = wide.shape
    for c in load_halves(move, m0, m1, t0, t1, slice(0, width), both, me):
        c.wait()
    step = d // pieces
    for p in range(pieces):
        wide[p * step:(p + 1) * step, :] = placed(both.at[0], p, code, pieces).astype(F32)
    move.store(wide, ghw_h.at[:, k * width:(k + 1) * width])
    for p in range(pieces):
        whole[p * step:(p + 1) * step, :] = placed(both.at[1], p, code, pieces)
    for c in range(0, width, 128):
        cs = slice(c, c + 128)
        tall[cs, :] = whole[:, cs].T.astype(F32)
    move.store(tall, grw_h.at[k * width:(k + 1) * width])
    move.finish()


def finish_ffn(meta, pieces, parts, k, shard, before, after=()):
    d, width = 2 * parts[0].shape[0], parts[0].shape[1]
    args = (meta, *parts, *before)
    return call(functools.partial(finish_ffn_kernel, pieces, k), "finish_ffn", args, "shhhh" + "h" * len(before),
                [("h", S((d, shard), F32)), ("h", S((shard, d), F32))],
                [VM((2, d, width), BF), VM((d, width), BF), VM((d, width), F32), VM((width, d), F32)], 8, 0, 4 * MIB,
                {5 + i: i for i in range(len(before))}, after)


def finish_pair_kernel(pieces, meta, m0, m1, t0, t1, *refs):
    outs, (both, wide, sems) = refs[:-3], refs[-3:]
    move = Mover(sems)
    me = meta[0]
    d = wide.shape[1]
    pairs = len(outs) // 2
    loads = [load_halves(move, m0, m1, t0, t1, slice(k * d, (k + 1) * d), both.at[k], me) for k in range(pairs)]
    step = d // pieces
    for k in range(pairs):
        for c in loads[k]:
            c.wait()
        for t in range(2):
            code = jnp.where(me == t, meta[2], meta[3])
            for p in range(pieces):
                wide[2 * k + t, p * step:(p + 1) * step, :] = placed(both.at[k, t], p, code, pieces).astype(F32)
            move.store(wide.at[2 * k + t], outs[2 * k + t])
    move.finish()


def finish_pair(meta, pieces, parts, d, after=()):
    pairs = parts[0].shape[1] // d
    return call(functools.partial(finish_pair_kernel, pieces), "finish_pair", (meta, *parts), "shhhh",
                [("h", S((d, d), F32))] * (2 * pairs), [VM((pairs, 2, d, d), BF), VM((2 * pairs, d, d), F32)], 4 + 6 * pairs, 0, 8 * MIB, None, after)


def bits_below(size):
    return [1 << i for i in range(size.bit_length() - 1)]


class Layout:
    def __init__(self, mesh):
        self.nb, self.nt = mesh.shape["batch"], mesh.shape["tp"]
        self.tp = [("tp", b) for b in reversed(bits_below(self.nt))]
        self.batch = [("batch", b) for b in bits_below(self.nb)[1:]]
        self.lanes = (self.tp + self.batch, self.batch[:1] + self.tp + self.batch[1:])

    def partner(self, device, level):
        b, t = divmod(device, self.nt)
        axis, bit = level
        return (b ^ bit) * self.nt + t if axis == "batch" else b * self.nt + (t ^ bit)

    def swap(self, value, level):
        pairs = []
        for device in range(self.nb * self.nt):
            core, to = device // self.nt % 2, device
            for one in level if isinstance(level, list) else [level]:
                to = self.partner(to, self.lanes[core][one] if isinstance(one, int) else one)
            pairs.append((device, to))
        return lax.ppermute(value, ("batch", "tp"), pairs)


CORE = ("batch", 1)


def code_of(levels, place):
    out = jnp.int32(0)
    for axis, bit in levels:
        out = out * 2 + (place[axis] // bit) % 2
    return out


def add(a, b):
    return (a.astype(F32) + b.astype(F32)).astype(BF)


def scatter_levels(levels, rows, least=48):
    n = 0
    while n < len(levels) and rows % 32 == 0 and rows // 2 >= least:
        rows //= 2
        n += 1
    return n


class Chain:
    def __init__(self, lay, steps):
        self.lay, self.steps, self.result = lay, steps, None
        self.go(next(steps))

    def go(self, requests):
        self.sent = [v for v, _ in requests]
        self.here = [self.lay.swap(v, level) for v, level in requests]

    def step(self):
        try:
            self.go(self.steps.send(self.here))
        except StopIteration as end:
            self.result, self.sent, self.here = end.value, [], []
        return self


def fence(arrays, *chains):
    chains = [c for c in chains if c.here]
    arrays, held = lax.optimization_barrier((arrays, [c.here for c in chains]))
    for chain, here in zip(chains, held):
        chain.here = here
        chain.step()
    return arrays


def sent(*chains):
    return tuple(v for c in chains for v in c.sent)


def halving(a, b, levels):
    for level in levels:
        n = a.shape[0] // 2
        kept = add(a[:n], b[:n])
        (b,) = yield [(add(a[n:], b[n:]), level)]
        a = kept
    return a, b


def quartering(a, b, high, low):
    n = a.shape[0] // 4
    parts = [add(a[i * n:(i + 1) * n], b[i * n:(i + 1) * n]) for i in range(4)]
    got = yield [(parts[1], [low]), (parts[2], [high]), (parts[3], [high, low])]
    return sum((g.astype(F32) for g in got), parts[0].astype(F32)).astype(BF)


def fourfold(held, high, low):
    got = yield [(held, [low]), (held, [high]), (held, [high, low])]
    return jnp.concatenate([held] + got, axis=0)


def doubling(held, levels):
    for level in levels:
        (got,) = yield [(held, level)]
        held = jnp.concatenate([held, got], axis=0)
    return held


def spread(held, level):
    other, mine = yield [(held, level), (held, CORE)]
    (rest,) = yield [(other, CORE)]
    return held, other, mine, rest


def reduce_ffn(lay, gone, stay, keep):
    m = len(lay.lanes[0])
    n = gone.shape[0]
    (recv,) = yield [(gone, CORE)]
    b, recv = yield [(add(keep[n:], recv), 0), (stay, CORE)]
    a, b = yield from halving(add(keep[:n], recv), b, range(1, m - 2))
    held = yield from quartering(a, b, m - 2, m - 1)
    held = yield from doubling(held, reversed(lay.batch[1:]))
    return (yield from spread(held, lay.batch[0]))


def reduce_pair(lay, n, send, keep, ahead):
    (recv,) = yield [(send, CORE)]
    if ahead:
        held = add(*(yield from halving(keep, recv, range(n))))
    else:
        a, b = yield from halving(keep, recv, range(n - 2))
        held = yield from quartering(a, b, n - 2, n - 1)
    for level in range(n, len(lay.lanes[0])):
        (got,) = yield [(held, level)]
        held = add(held, got)
    return held


def gather_pairs(lay, n, held):
    held = yield from fourfold(held, n - 2, n - 1)
    held = yield from doubling(held, reversed(range(1, n - 2)))
    return (yield from spread(held, 0))


def reduce_small(lay, vectors, hidden):
    n, shard = vectors.shape[0], hidden[0].shape[0]
    for level in lay.tp:
        bit = level[1]
        (got,) = yield [(jnp.concatenate([vectors] + [hidden[j + bit] for j in range(bit)]), level)]
        vectors = vectors + got[:n]
        hidden = [hidden[j] + got[n + j * shard:n + (j + 1) * shard] for j in range(bit)]
    held = jnp.concatenate([vectors, hidden[0]])
    for level in [CORE] + lay.batch[:-2]:
        (got,) = yield [(held, level)]
        held = held + got
    high, low = lay.batch[-2:]
    got = yield [(held, [low]), (held, [high]), (held, [high, low])]
    return held + got[0] + got[1] + got[2]


def on_device(
    lay,
    inputs,
    cotangent,
    zinc_lengths,
    pubchem_lengths,
    feature_stack,
    train_step,
    redraw_interval,
    attn_gain,
    attn_shift,
    query_weight,
    query_bias,
    key_weight,
    key_bias,
    value_weight,
    value_bias,
    output_weight,
    output_bias,
    ffn_gain,
    ffn_shift,
    hidden_weight,
    hidden_bias,
    return_weight,
    return_bias,
):
    nt = lay.nt
    d, shard = hidden_weight.shape
    rows = inputs.shape[0]
    width = min(768, shard)
    chunks = shard // width
    zm, pm = zinc_lengths.shape[0], pubchem_lengths.shape[0]
    place = {"batch": lax.axis_index("batch"), "tp": lax.axis_index("tp")}
    core = place["batch"] % 2

    def shares(k):
        hw = lax.dynamic_slice(hidden_weight, (core * (d // 2), k * width), (d // 2, width))
        rw = lax.dynamic_slice(return_weight, (k * width + core * (width // 2), 0), (width // 2, d))
        return [jnp.concatenate([hw, rw], axis=0)] if width == d else [hw, rw]

    def from_tp(own):
        pool = {0: own}
        for level in lay.tp:
            for j in list(pool):
                pool[j | level[1]] = [lay.swap(v, level) for v in pool[j]]
        return [v for j in range(1, nt) for v in pool[j]]

    own = [shares(k) for k in range(chunks)]
    per = len(own[0])
    biases = from_tp([hidden_bias])
    here = {k: from_tp(own[k]) for k in range(chunks)}

    n_pair = scatter_levels(lay.lanes[0], d)
    codes = [code_of(lane[:n_pair], place) for lane in lay.lanes]
    pick = train_step[0] // redraw_interval[0] % feature_stack.shape[0]
    meta = jnp.stack([core, code_of(lay.batch, place), jnp.where(core == 0, codes[0], codes[1]), jnp.where(core == 0, codes[1], codes[0]),
                      code_of(lay.batch[:-2], place) * 4, pick]).astype(jnp.int32)
    table = rotary_const()

    out = attend_fwd(
        meta, zinc_lengths, pubchem_lengths, cotangent, inputs,
        (attn_gain, attn_shift, query_bias, key_bias, value_bias, output_bias, ffn_gain, ffn_shift),
        query_weight, key_weight, value_weight, output_weight, feature_stack, table)
    out, here[0], biases = lax.optimization_barrier((out, here[0], biases))
    qkv, f, state, trans, middle, n2, left, proj = out

    pieces, pair_pieces = 2 ** len(lay.batch), 2 ** n_pair
    chains, acts, rws, hidden, before = [], [], [], [], ()
    for k in range(chunks):
        if chains:
            here[k] = fence(here[k], chains[-1])
        near = [lay.swap(v, CORE) for v in here[k]]
        parts = [[v[i] for i in range(j * per, (j + 1) * per) for v in (here[k], near)] for j in range(nt - 1)]
        out = ffn_chunk(meta, pieces, nt, n2, left, cotangent, hidden_bias, hidden_weight, return_weight, parts, biases, k, width,
                        before, sent(*chains))
        gone, stay, keep, act, bias, e, rw = fence(out, *chains)
        before = (e,)
        chains.append(Chain(lay, reduce_ffn(lay, gone, stay, keep)))
        acts.append(act)
        rws.append(rw)
        hidden.append(bias)

    middle = fence(middle, chains[-1])
    out = mid(e, cotangent, middle, output_weight, ffn_gain, sent(*chains))
    gm, gb, gatt, vec1 = fence(out, *chains[:-1])
    out = value_bwd(meta, zm, pm, pair_pieces, gatt, gb, f, state, trans, sent(*chains))
    send, keep, gv, uw, gst, vec2 = fence(out, *chains)
    pair_a = Chain(lay, reduce_pair(lay, n_pair, send, keep, True))
    uw = fence(uw, pair_a)
    out = query_bwd(meta, zm, pm, pair_pieces, uw, gst, qkv, f, state, trans, proj, table, sent(pair_a, *chains))
    send, keep, gqk, vec3 = fence(out, pair_a, *chains)
    pair_b = Chain(lay, reduce_pair(lay, n_pair, send, keep, False))
    gqk = fence(gqk, pair_b)
    out = input_back(gqk, gv, query_weight, key_weight, value_weight, inputs, gm, attn_gain, sent(pair_a, pair_b, *chains))
    (input_grad, vec4), middle = fence((out, middle), pair_a, pair_b, *chains)
    layer_out = layer_end(acts, rws, middle, return_bias, sent(pair_b, pair_a, *chains))
    layer_out, vec4 = fence((layer_out, vec4), pair_b, pair_a, *chains)
    vec3 = jnp.concatenate([vec3, vec4], axis=0)
    vectors = jnp.concatenate([vec1, vec2, vec3], axis=0).reshape(-1)
    small = Chain(lay, reduce_small(lay, vectors, [jnp.concatenate([hidden[k][j] for k in range(chunks)]) for j in range(nt)]))

    ffn_out, k, pairs = (), 0, None
    while pairs is None or pairs.here or any(c.here for c in chains):
        every = [pairs] if pairs else [pair_b, pair_a]
        every += chains + [small]
        if k < chunks and chains[k].result is not None:
            ffn_out = finish_ffn(meta, pieces, chains[k].result, k, shard, ffn_out, sent(*every))
            k += 1
            ffn_out = fence(ffn_out, *every)
        else:
            fence((), *every)
        if pairs is None and pair_a.result is not None and pair_b.result is not None:
            pairs = Chain(lay, gather_pairs(lay, n_pair, jnp.concatenate([pair_a.result, pair_b.result], axis=1)))
    while k < chunks:
        ffn_out = finish_ffn(meta, pieces, chains[k].result, k, shard, ffn_out, sent(small))
        k += 1
    while small.here:
        small.step()
    gwo, gwv, gwq, gwk = finish_pair(meta, pair_pieces, pairs.result, d, (small.result,))
    vecs = small.result[:9 * d].reshape(9, d)
    return (layer_out, input_grad, vecs[7], vecs[8], gwq, vecs[5], gwk, vecs[6], gwv, vecs[4], gwo, vecs[2],
            vecs[0], vecs[1], ffn_out[0], small.result[9 * d:], ffn_out[1], vecs[3])


def solution(mesh):
    rows, whole, hidden = P(("batch", "tp"), None), P(), P(None, "tp")
    return jax.shard_map(
        functools.partial(on_device, Layout(mesh)),
        mesh=mesh,
        in_specs=(rows, rows, P(("batch", "tp")), P(("batch", "tp"))) + (whole,) * 15 + (hidden, P("tp"), P("tp", None), whole),
        out_specs=(rows, rows) + (whole,) * 12 + (hidden, P("tp"), P("tp", None), whole),
        check_vma=False,
    )
```

profile of v0, /device:TPU:0, one launch (start us, length us, event | category | flops | bytes accessed | tf_op | source)
XLA Modules:
  0.0 245.6 jit_solution(14979386828172530181)
XLA Ops:
  0.7 1.8 constant_dynamic-slice_fusion
  2.7 3.0 %collective-permute-start = (bf16[768,768]{1,0:T(8,128)(2,1)S(1)}, bf16[768,768]{1,0:T(8,128)(2,1)}, u32[]{:S(2)}, u32[]{:S(2)}) collective-permute-start(bf16[768,768]{1,0:T(8,128)(2,1)S(1)} %pad_maximum_fusion), channel_id=1, source_target_pairs={{0,1},{1,0},{2,3},{3,2},{4,5},{5,4},{6,7},{7,6},{8,9},{9,8},{10,11... | collective-permute-start | bytes 3538952 | tf_op jit(solution)/shard_map/ppermute | solution.py:680
  7.7 23.7 %attend_fwd.1 = (bf16[3,768,768]{2,1,0:T(8,128)(2,1)}, bf16[2,768,384]{2,1,0:T(8,128)(2,1)S(1)}, bf16[6,3,128,512]{3,2,1,0:T(8,128)(2,1)}, bf16[2,768,768]{2,1,0...) custom-call(s32[6]{0:T(128)S(1)} %stack.27.refs_0_, ...), custom_call_target="tpu_custom_call" | custom-call | flops 27599998976 | bytes 16777216 | tf_op jit(solution)/shard_map/attend_fwd/pallas_call | solution.py:94
  32.5 1.6 collective-permute-start.2
  35.9 17.5 %ffn_chunk.2 = (bf16[768,768]{1,0:T(8,128)(2,1)S(1)}, bf16[768,768]{1,0:T(8,128)(2,1)}, bf16[1536,768]{1,0:T(8,128)(2,1)}, bf16[2,768,768]{2,1,0:T(8,128)(2,1)},...) custom-call(s32[6]{0:T(128)S(1)} %stack.27.refs_0_, ...), custom_call_target="tpu_custom_call" | custom-call | flops 19549999104 | bytes 12582912 | tf_op jit(solution)/shard_map/ffn_chunk/pallas_call | solution.py:94
  53.6 6.8 %collective-permute-done.2.refs_7_ = bf16[768,768]{1,0:T(8,128)(2,1)S(1)} collective-permute-done((bf16[768,768]{1,0:T(8,128)(2,1)S(1)}, bf16[768,768]{1,0:T(8,128)(2,1)S(1)}, u32[]{:S(2)}, u32[]{:S(2)}) %collective-permute-start.2) | collective-permute-done | bytes 1179680 | tf_op jit(solution)/shard_map/ppermute | solution.py:680
  60.9 1.6 add_convert_fusion.3.refs_11_
  62.5 1.8 collective-permute-start.6
  65.4 17.5 %ffn_chunk.3 = (bf16[768,768]{1,0:T(8,128)(2,1)S(1)}, bf16[768,768]{1,0:T(8,128)(2,1)}, bf16[1536,768]{1,0:T(8,128)(2,1)}, bf16[2,768,768]{2,1,0:T(8,128)(2,1)},...) custom-call(s32[6]{0:T(128)S(1)} %stack.27.refs_0_, ...), custom_call_target="tpu_custom_call" | custom-call | flops 19549999104 | bytes 12582912 | tf_op jit(solution)/shard_map/ffn_chunk/pallas_call | solution.py:94
  83.6 1.8 collective-permute-start.9
  86.1 1.7 collective-permute-start.13
  87.8 6.1 %mid.1 = (f32[768,768]{1,0:T(8,128)}, bf16[768,768]{1,0:T(8,128)(2,1)S(1)}, bf16[768,768]{1,0:T(8,128)(2,1)}, f32[4,768]{1,0:T(4,128)S(1)}) custom-call(f32[768,768]{1,0:T(8,128)} %get-tuple-element.180.refs_0_, bf16[768,768]{1,0:T(8,128)(2,1)} %refs_1_.4, f32[768,768]{1,0:T(8,128)} %get-tuple-element.234.refs_2_.refs_0_, bf16[768,768]{1,0:T(8,128)(2,1)} %refs_3_.8, ...), custom_call_target="tpu_custom_call" | custom-call | flops 9200000000 | bytes 8388608 | tf_op jit(solution)/shard_map/mid/pallas_call | solution.py:94
  94.9 3.2 %collective-permute-done.9 = bf16[384,768]{1,0:T(8,128)(2,1)S(1)} collective-permute-done((bf16[384,768]{1,0:T(8,128)(2,1)S(1)}, bf16[384,768]{1,0:T(8,128)(2,1)S(1)}, u32[]{:S(2)}, u32[]{:S(2)}) %collective-permute-start.9) | collective-permute-done | bytes 589856 | tf_op jit(solution)/shard_map/ppermute | solution.py:680
  98.2 3.0 %collective-permute-start.10 = (bf16[96,768]{1,0:T(8,128)(2,1)S(1)}, bf16[96,768]{1,0:T(8,128)(2,1)S(1)}, u32[]{:S(2)}, u32[]{:S(2)}) collective-permute-start(bf16[96,768]{1,0:T(8,128)(2,1)S(1)} %get-tuple-element.317.refs_6_), channel_id=1, source_target_pairs={{0,16},{1,17},{2,18},{3,19},{4,20},{5,21},{6,22},{7,23},{8,24},{9,... | collective-permute-start | bytes 442376 | tf_op jit(solution)/shard_map/ppermute | solution.py:680
  101.2 1.6 collective-permute-start.11
  102.8 12.7 %value_bwd.1 = (bf16[768,768]{1,0:T(8,128)(2,1)S(1)}, bf16[768,768]{1,0:T(8,128)(2,1)}, bf16[768,768]{1,0:T(8,128)(2,1)}, bf16[768,1536]{1,0:T(8,128)(2,1)}, bf1...) custom-call(s32[6]{0:T(128)S(1)} %stack.27.refs_0_, bf16[768,768]{1,0:T(8,128)(2,1)} %get-tuple-element.193.refs_1_, ...), custom_call_target="tpu_custom_call" | custom-call | flops 14949999616 | bytes 8388608 | tf_op jit(solution)/shard_map/value_bwd/pallas_call | solution.py:94
  116.3 1.8 collective-permute-start.18
  118.2 1.8 collective-permute-start.17
  120.3 1.6 collective-permute-start.16
  121.8 12.0 %query_bwd.1 = (bf16[768,768]{1,0:T(8,128)(2,1)}, bf16[768,768]{1,0:T(8,128)(2,1)}, bf16[2,768,768]{2,1,0:T(8,128)(2,1)}, f32[2,768]{1,0:T(2,128)S(1)}) custom-call(s32[6]{0:T(128)S(1)} %stack.27.refs_0_, bf16[768,1536]{1,0:T(8,128)(2,1)} %get-tuple-element.207.refs_1_, bf16[6,3,128,512]{3,2,1,0:T(8,128)(2,1)} %get-tuple-element.208.refs_2_, ...), custom_call_target="tpu_custom_call" | custom-call | flops 14949999616 | bytes 12582912 | tf_op jit(solution)/shard_map/query_bwd/pallas_call | solution.py:94
  134.2 1.3 collective-permute-start.23
  135.5 1.7 collective-permute-start.24
  137.2 1.9 collective-permute-start.25
  141.3 3.6 %collective-permute-done.23 = bf16[96,768]{1,0:T(8,128)(2,1)S(1)} collective-permute-done((bf16[96,768]{1,0:T(8,128)(2,1)S(1)}, bf16[96,768]{1,0:T(8,128)(2,1)S(1)}, u32[]{:S(2)}, u32[]{:S(2)}) %collective-permute-start.23) | collective-permute-done | bytes 147488 | tf_op jit(solution)/shard_map/ppermute | solution.py:680
  145.5 9.0 %input_back.1 = (bf16[768,768]{1,0:T(8,128)(2,1)}, f32[2,768]{1,0:T(2,128)S(1)}) custom-call(bf16[2,768,768]{2,1,0:T(8,128)(2,1)} %get-tuple-element.224.refs_0_, bf16[768,768]{1,0:T(8,128)(2,1)} %get-tuple-element.225.refs_1_, bf16[768,768]{1,0:T(8,128)(2,1)} %refs_2_.3, bf16[768,768]{1,0:T(8,128)(2,1)} %refs_3_.9, bf16[768,768]{1,0:T(8,128)(2,1)} %refs_4_.5, ...), custom_call_target="tpu_custom_call" | custom-call | flops 11500000256 | bytes 8388608 | tf_op jit(solution)/shard_map/input_back/pallas_call | solution.py:94
  155.9 1.5 collective-permute-start.30
  157.5 3.7 %collective-permute-start.27 = (bf16[96,768]{1,0:T(8,128)(2,1)S(1)}, bf16[96,768]{1,0:T(8,128)(2,1)S(1)}, u32[]{:S(2)}, u32[]{:S(2)}) collective-permute-start(bf16[96,768]{1,0:T(8,128)(2,1)S(1)} %get-tuple-element.319.refs_7_), channel_id=1, source_target_pairs={{0,8},{1,9},{2,10},{3,11},{4,12},{5,13},{6,14},{7,15},{8,0},{9,1},... | collective-permute-start | bytes 442376 | tf_op jit(solution)/shard_map/ppermute | solution.py:680
  161.5 9.6 %layer_end.1 = bf16[768,768]{1,0:T(8,128)(2,1)} custom-call(f32[768,768]{1,0:T(8,128)} %get-tuple-element.234.refs_2_.refs_0_, f32[768]{0:T(1024)S(1)} %copy-done.12, bf16[2,768,768]{2,1,0:T(8,128)(2,1)} %get-tuple-element.235.refs_2_, bf16[2,768,768]{2,1,0:T(8,128)(2,1)} %get-tuple-element.236.refs_3_, bf16[2,768,768]{2,1,0:T(8,128)(2,1)} %get-tuple-element.237.refs_4_, ...), custom_call_target="tpu_custom_call" | custom-call | flops 10350000128 | bytes 12582912 | tf_op jit(solution)/shard_map/layer_end/pallas_call | solution.py:94
  171.2 1.4 collective-permute-done.26
  173.8 3.6 %collective-permute-start.34 = (bf16[48,768]{1,0:T(8,128)(2,1)S(1)}, bf16[48,768]{1,0:T(8,128)(2,1)S(1)}, u32[]{:S(2)}, u32[]{:S(2)}) collective-permute-start(bf16[48,768]{1,0:T(8,128)(2,1)S(1)} %add_convert_fusion.32), channel_id=1, source_target_pairs={{0,16},{1,17},{2,18},{3,19},{4,20},{5,21},{6,22},{7,23},{8,24},{9,... | collective-permute-start | bytes 221192 | tf_op jit(solution)/shard_map/ppermute | solution.py:680
  178.5 4.2 %collective-permute-done.34 = bf16[48,768]{1,0:T(8,128)(2,1)S(1)} collective-permute-done((bf16[48,768]{1,0:T(8,128)(2,1)S(1)}, bf16[48,768]{1,0:T(8,128)(2,1)S(1)}, u32[]{:S(2)}, u32[]{:S(2)}) %collective-permute-start.34) | collective-permute-done | bytes 73760 | tf_op jit(solution)/shard_map/ppermute | solution.py:680
  182.7 3.2 %collective-permute-start.33 = (bf16[48,768]{1,0:T(8,128)(2,1)S(1)}, bf16[48,768]{1,0:T(8,128)(2,1)S(1)}, u32[]{:S(2)}, u32[]{:S(2)}) collective-permute-start(bf16[48,768]{1,0:T(8,128)(2,1)S(1)} %get-tuple-element.320), channel_id=1, source_target_pairs={{0,24},{1,25},{2,26},{3,27},{4,28},{5,29},{6,30},{7,31},{8,16},{9,... | collective-permute-start | bytes 221192 | tf_op jit(solution)/shard_map/ppermute | solution.py:680
  185.9 1.6 collective-permute-done.32
  187.5 3.4 %collective-permute-done.33 = bf16[48,768]{1,0:T(8,128)(2,1)S(1)} collective-permute-done((bf16[48,768]{1,0:T(8,128)(2,1)S(1)}, bf16[48,768]{1,0:T(8,128)(2,1)S(1)}, u32[]{:S(2)}, u32[]{:S(2)}) %collective-permute-start.33) | collective-permute-done | bytes 73760 | tf_op jit(solution)/shard_map/ppermute | solution.py:680
  194.5 2.2 collective-permute-start.40
  196.7 4.7 %finish_ffn.2 = (f32[768,1536]{1,0:T(8,128)}, f32[1536,768]{1,0:T(8,128)}) custom-call(s32[6]{0:T(128)S(1)} %stack.27.refs_0_, bf16[384,768]{1,0:T(8,128)(2,1)S(1)} %pad_maximum_fusion.2.refs_8_.refs_9_.refs_1_, bf16[384,768]{1,0:T(8,128)(2,1)S(1)} %collective-permute-done.28.refs_2_, bf16[384,768]{1,0:T(8,128)(2,1)S(1)} %collective-permute-done.29.refs_3_, ...), custom_call_target="tpu_custom_call" | custom-call | flops 5750000128 | bytes 4194304 | tf_op jit(solution)/shard_map/finish_ffn/pallas_call | solution.py:94
  201.4 2.4 collective-permute-done.38
  203.9 2.3 collective-permute-done.40
  206.2 1.6 collective-permute-start.46
  208.4 1.8 collective-permute-done.46
  210.2 7.6 %collective-permute-done.44 = bf16[192,1536]{1,0:T(8,128)(2,1)S(1)} collective-permute-done((bf16[192,1536]{1,0:T(8,128)(2,1)S(1)}, bf16[192,1536]{1,0:T(8,128)(2,1)S(1)}, u32[]{:S(2)}, u32[]{:S(2)}) %collective-permute-start.44) | collective-permute-done | bytes 589856 | tf_op jit(solution)/shard_map/ppermute | solution.py:680
  217.8 1.5 collective-permute-start.47
  219.4 2.9 %collective-permute-start.49 = (f32[8448]{0:T(1024)S(1)}, f32[8448]{0:T(1024)S(1)}, u32[]{:S(2)}, u32[]{:S(2)}) collective-permute-start(f32[8448]{0:T(1024)S(1)} %add.278.refs_9_.refs_10_.refs_11_), channel_id=1, source_target_pairs={{0,16},{1,17},{2,18},{3,19},{4,20},{5,21},{6,22},{7,23},{8,24},{9,... | collective-permute-start | bytes 101384 | tf_op jit(solution)/shard_map/ppermute | solution.py:680
  222.4 2.3 collective-permute-start.51
  224.7 4.7 %finish_ffn.3 = (f32[768,1536]{1,0:T(8,128)}, f32[1536,768]{1,0:T(8,128)}) custom-call(s32[6]{0:T(128)S(1)} %stack.27.refs_0_, bf16[384,768]{1,0:T(8,128)(2,1)S(1)} %copy-done.1, bf16[384,768]{1,0:T(8,128)(2,1)S(1)} %collective-permute-done.41.refs_2_, ...), custom_call_target="tpu_custom_call", output_to_operand_aliasing={{0}: (5, {}), {1}: (6, {})} | custom-call | flops 5750000128 | bytes 4194304 | tf_op jit(solution)/shard_map/finish_ffn/pallas_call | solution.py:94
  229.4 4.7 %collective-permute-done.47.refs_2_ = bf16[384,1536]{1,0:T(8,128)(2,1)S(1)} collective-permute-done((bf16[384,1536]{1,0:T(8,128)(2,1)S(1)}, bf16[384,1536]{1,0:T(8,128)(2,1)S(1)}, u32[]{:S(2)}, u32[]{:S(2)}) %collective-permute-start.47) | collective-permute-done | bytes 1179680 | tf_op jit(solution)/shard_map/ppermute | solution.py:680
  235.5 1.5 collective-permute-done.52.refs_4_
  239.3 6.0 %finish_pair.1 = (f32[768,768]{1,0:T(8,128)}, f32[768,768]{1,0:T(8,128)}, f32[768,768]{1,0:T(8,128)}, f32[768,768]{1,0:T(8,128)}) custom-call(s32[6]{0:T(128)S(1)} %stack.27.refs_0_, bf16[384,1536]{1,0:T(8,128)(2,1)S(1)} %copy-done.3, bf16[384,1536]{1,0:T(8,128)(2,1)} %copy-done.29, bf16[384,1536]{1,0:T(8,128)(2,1)} %copy-done.30, ...), custom_call_target="tpu_custom_call" | custom-call | flops 5750000128 | bytes 8388608 | tf_op jit(solution)/shard_map/finish_pair/pallas_call | solution.py:94
  (191 shorter events, 24.0 us)
Async XLA Ops:
  2.7 29.2 %collective-permute-start = (bf16[768,768]{1,0:T(8,128)(2,1)S(1)}, bf16[768,768]{1,0:T(8,128)(2,1)}, u32[]{:S(2)}, u32[]{:S(2)}) collective-permute-start(bf16[768,768]{1,0:T(8,128)(2,1)S(1)} %pad_maximum_fusion), channel_id=1, source_target_pairs={{0,1},{1,0},{2,3},{3,2},{4,5},{5,4},{6,7},{7,6},{8,9},{9,8},{10,11... | collective-permute-start | bytes 3538952 | tf_op jit(solution)/shard_map/ppermute | solution.py:680
  5.7 26.1 %collective-permute-start.1 = (bf16[1536]{0:T(1024)(128)(2,1)S(1)}, bf16[1536]{0:T(1024)(128)(2,1)S(1)}, u32[]{:S(2)}, u32[]{:S(2)}) collective-permute-start(bf16[1536]{0:T(1024)(128)(2,1)S(1)} %copy-done.27), channel_id=1, source_target_pairs={{0,1},{1,0},{2,3},{3,2},{4,5},{5,4},{6,7},{7,6},{8,9},{9,8},{10,11... | collective-permute-start | bytes 9224 | tf_op jit(solution)/shard_map/ppermute | solution.py:680
  32.5 27.9 %collective-permute-start.2 = (bf16[768,768]{1,0:T(8,128)(2,1)S(1)}, bf16[768,768]{1,0:T(8,128)(2,1)S(1)}, u32[]{:S(2)}, u32[]{:S(2)}) collective-permute-start(bf16[768,768]{1,0:T(8,128)(2,1)S(1)} %pad_maximum_fusion.1), channel_id=1, source_target_pairs={{0,1},{1,0},{2,3},{3,2},{4,5},{5,4},{6,7},{7,6},{8,9},{9,8},{10,11... | collective-permute-start | bytes 3538952 | tf_op jit(solution)/shard_map/ppermute | solution.py:680
  53.4 7.0 %collective-permute-start.4 = (bf16[768,768]{1,0:T(8,128)(2,1)S(1)}, bf16[768,768]{1,0:T(8,128)(2,1)S(1)}, u32[]{:S(2)}, u32[]{:S(2)}) collective-permute-start(bf16[768,768]{1,0:T(8,128)(2,1)S(1)} %get-tuple-element.167), channel_id=1, source_target_pairs={{0,2},{1,3},{2,0},{3,1},{4,6},{5,7},{6,4},{7,5},{8,10},{9,11},{10,... | collective-permute-start | bytes 3538952 | tf_op jit(solution)/shard_map/ppermute | solution.py:680
  60.4 22.5 %collective-permute-start.7 = (bf16[768,768]{1,0:T(8,128)(2,1)}, bf16[768,768]{1,0:T(8,128)(2,1)S(1)}, u32[]{:S(2)}, u32[]{:S(2)}) collective-permute-start(bf16[768,768]{1,0:T(8,128)(2,1)} %get-tuple-element.172.refs_12_), channel_id=1, source_target_pairs={{0,2},{1,3},{2,0},{3,1},{4,6},{5,7},{6,4},{7,5},{8,10},{9,11},{10,... | collective-permute-start | bytes 3538952 | tf_op jit(solution)/shard_map/ppermute | solution.py:680
  62.5 20.3 %collective-permute-start.6 = (bf16[768,768]{1,0:T(8,128)(2,1)S(1)}, bf16[768,768]{1,0:T(8,128)(2,1)S(1)}, u32[]{:S(2)}, u32[]{:S(2)}) collective-permute-start(bf16[768,768]{1,0:T(8,128)(2,1)S(1)} %add_convert_fusion.3.refs_11_), channel_id=1, source_target_pairs={{0,1},{1,0},{2,6},{3,7},{4,5},{5,4},{6,2},{7,3},{8,9},{9,8},{10,14... | collective-permute-start | bytes 3538952 | tf_op jit(solution)/shard_map/ppermute | solution.py:680
  83.6 14.5 %collective-permute-start.9 = (bf16[384,768]{1,0:T(8,128)(2,1)S(1)}, bf16[384,768]{1,0:T(8,128)(2,1)S(1)}, u32[]{:S(2)}, u32[]{:S(2)}) collective-permute-start(bf16[384,768]{1,0:T(8,128)(2,1)S(1)} %get-tuple-element.303.refs_5_), channel_id=1, source_target_pairs={{0,4},{1,5},{2,3},{3,2},{4,0},{5,1},{6,7},{7,6},{8,12},{9,13},{10,... | collective-permute-start | bytes 1769480 | tf_op jit(solution)/shard_map/ppermute | solution.py:680
  85.4 30.1 %collective-permute-start.14 = (bf16[768,768]{1,0:T(8,128)(2,1)S(1)}, bf16[768,768]{1,0:T(8,128)(2,1)S(1)}, u32[]{:S(2)}, u32[]{:S(2)}) collective-permute-start(bf16[768,768]{1,0:T(8,128)(2,1)S(1)} %copy-done.28), channel_id=1, source_target_pairs={{0,2},{1,3},{2,0},{3,1},{4,6},{5,7},{6,4},{7,5},{8,10},{9,11},{10,... | collective-permute-start | bytes 3538952 | tf_op jit(solution)/shard_map/ppermute | solution.py:680
  86.1 29.4 %collective-permute-start.13 = (bf16[768,768]{1,0:T(8,128)(2,1)S(1)}, bf16[768,768]{1,0:T(8,128)(2,1)S(1)}, u32[]{:S(2)}, u32[]{:S(2)}) collective-permute-start(bf16[768,768]{1,0:T(8,128)(2,1)S(1)} %add_convert_fusion.1.refs_6_.refs_9_), channel_id=1, source_target_pairs={{0,1},{1,0},{2,6},{3,7},{4,5},{5,4},{6,2},{7,3},{8,9},{9,8},{10,14... | collective-permute-start | bytes 3538952 | tf_op jit(solution)/shard_map/ppermute | solution.py:680
  98.2 17.3 %collective-permute-start.10 = (bf16[96,768]{1,0:T(8,128)(2,1)S(1)}, bf16[96,768]{1,0:T(8,128)(2,1)S(1)}, u32[]{:S(2)}, u32[]{:S(2)}) collective-permute-start(bf16[96,768]{1,0:T(8,128)(2,1)S(1)} %get-tuple-element.317.refs_6_), channel_id=1, source_target_pairs={{0,16},{1,17},{2,18},{3,19},{4,20},{5,21},{6,22},{7,23},{8,24},{9,... | collective-permute-start | bytes 442376 | tf_op jit(solution)/shard_map/ppermute | solution.py:680
  101.2 14.3 %collective-permute-start.11 = (bf16[96,768]{1,0:T(8,128)(2,1)S(1)}, bf16[96,768]{1,0:T(8,128)(2,1)S(1)}, u32[]{:S(2)}, u32[]{:S(2)}) collective-permute-start(bf16[96,768]{1,0:T(8,128)(2,1)S(1)} %get-tuple-element.316.refs_7_), channel_id=1, source_target_pairs={{0,8},{1,9},{2,10},{3,11},{4,12},{5,13},{6,14},{7,15},{8,0},{9,1},... | collective-permute-start | bytes 442376 | tf_op jit(solution)/shard_map/ppermute | solution.py:680
  102.8 12.7 %collective-permute-start.12 = (bf16[96,768]{1,0:T(8,128)(2,1)S(1)}, bf16[96,768]{1,0:T(8,128)(2,1)S(1)}, u32[]{:S(2)}, u32[]{:S(2)}) collective-permute-start(bf16[96,768]{1,0:T(8,128)(2,1)S(1)} %get-tuple-element.315.refs_8_), channel_id=1, source_target_pairs={{0,24},{1,25},{2,26},{3,27},{4,28},{5,29},{6,30},{7,31},{8,16},{9,... | collective-permute-start | bytes 442376 | tf_op jit(solution)/shard_map/ppermute | solution.py:680
  115.6 4.4 %collective-permute-start.15 = (bf16[768,768]{1,0:T(8,128)(2,1)S(1)}, bf16[768,768]{1,0:T(8,128)(2,1)S(1)}, u32[]{:S(2)}, u32[]{:S(2)}) collective-permute-start(bf16[768,768]{1,0:T(8,128)(2,1)S(1)} %get-tuple-element.206), channel_id=1, source_target_pairs={{0,2},{1,3},{2,0},{3,1},{4,6},{5,7},{6,4},{7,5},{8,10},{9,11},{10,... | collective-permute-start | bytes 3538952 | tf_op jit(solution)/shard_map/ppermute | solution.py:680
  116.3 17.6 %collective-permute-start.18 = (bf16[384,768]{1,0:T(8,128)(2,1)S(1)}, bf16[384,768]{1,0:T(8,128)(2,1)S(1)}, u32[]{:S(2)}, u32[]{:S(2)}) collective-permute-start(bf16[384,768]{1,0:T(8,128)(2,1)S(1)} %get-tuple-element.299.refs_12_), channel_id=1, source_target_pairs={{0,4},{1,5},{2,3},{3,2},{4,0},{5,1},{6,7},{7,6},{8,12},{9,13},{10,... | collective-permute-start | bytes 1769480 | tf_op jit(solution)/shard_map/ppermute | solution.py:680
  118.2 15.7 %collective-permute-start.17 = (bf16[96,768]{1,0:T(8,128)(2,1)S(1)}, bf16[96,768]{1,0:T(8,128)(2,1)S(1)}, u32[]{:S(2)}, u32[]{:S(2)}) collective-permute-start(bf16[96,768]{1,0:T(8,128)(2,1)S(1)} %add_convert_fusion.23.refs_11_), channel_id=1, source_target_pairs={{0,16},{1,17},{2,18},{3,19},{4,20},{5,21},{6,22},{7,23},{8,24},{9,... | collective-permute-start | bytes 442376 | tf_op jit(solution)/shard_map/ppermute | solution.py:680
  120.3 13.6 %collective-permute-start.16 = (bf16[384,768]{1,0:T(8,128)(2,1)S(1)}, bf16[384,768]{1,0:T(8,128)(2,1)S(1)}, u32[]{:S(2)}, u32[]{:S(2)}) collective-permute-start(bf16[384,768]{1,0:T(8,128)(2,1)S(1)} %get-tuple-element.301.refs_10_), channel_id=1, source_target_pairs={{0,1},{1,0},{2,6},{3,7},{4,5},{5,4},{6,2},{7,3},{8,9},{9,8},{10,14... | collective-permute-start | bytes 1769480 | tf_op jit(solution)/shard_map/ppermute | solution.py:680
  133.9 6.5 %collective-permute-start.19 = (bf16[768,768]{1,0:T(8,128)(2,1)}, bf16[768,768]{1,0:T(8,128)(2,1)S(1)}, u32[]{:S(2)}, u32[]{:S(2)}) collective-permute-start(bf16[768,768]{1,0:T(8,128)(2,1)} %get-tuple-element.223), channel_id=1, source_target_pairs={{0,2},{1,3},{2,0},{3,1},{4,6},{5,7},{6,4},{7,5},{8,10},{9,11},{10,... | collective-permute-start | bytes 3538952 | tf_op jit(solution)/shard_map/ppermute | solution.py:680
  134.2 10.8 %collective-permute-start.23 = (bf16[96,768]{1,0:T(8,128)(2,1)S(1)}, bf16[96,768]{1,0:T(8,128)(2,1)S(1)}, u32[]{:S(2)}, u32[]{:S(2)}) collective-permute-start(bf16[96,768]{1,0:T(8,128)(2,1)S(1)} %get-tuple-element.314.refs_11_), channel_id=1, source_target_pairs={{0,16},{1,17},{2,18},{3,19},{4,20},{5,21},{6,22},{7,23},{8,24},{9,... | collective-permute-start | bytes 442376 | tf_op jit(solution)/shard_map/ppermute | solution.py:680
  135.5 19.0 %collective-permute-start.24 = (bf16[96,768]{1,0:T(8,128)(2,1)S(1)}, bf16[96,768]{1,0:T(8,128)(2,1)S(1)}, u32[]{:S(2)}, u32[]{:S(2)}) collective-permute-start(bf16[96,768]{1,0:T(8,128)(2,1)S(1)} %get-tuple-element.313.refs_12_), channel_id=1, source_target_pairs={{0,8},{1,9},{2,10},{3,11},{4,12},{5,13},{6,14},{7,15},{8,0},{9,1},... | collective-permute-start | bytes 442376 | tf_op jit(solution)/shard_map/ppermute | solution.py:680
  137.2 17.4 %collective-permute-start.25 = (bf16[96,768]{1,0:T(8,128)(2,1)S(1)}, bf16[96,768]{1,0:T(8,128)(2,1)S(1)}, u32[]{:S(2)}, u32[]{:S(2)}) collective-permute-start(bf16[96,768]{1,0:T(8,128)(2,1)S(1)} %get-tuple-element.312.refs_13_), channel_id=1, source_target_pairs={{0,24},{1,25},{2,26},{3,27},{4,28},{5,29},{6,30},{7,31},{8,16},{9,... | collective-permute-start | bytes 442376 | tf_op jit(solution)/shard_map/ppermute | solution.py:680
  139.1 15.4 %collective-permute-start.22 = (bf16[192,768]{1,0:T(8,128)(2,1)S(1)}, bf16[192,768]{1,0:T(8,128)(2,1)S(1)}, u32[]{:S(2)}, u32[]{:S(2)}) collective-permute-start(bf16[192,768]{1,0:T(8,128)(2,1)S(1)} %pad_maximum_fusion.5.refs_10_), channel_id=1, source_target_pairs={{0,8},{1,9},{2,10},{3,11},{4,12},{5,13},{6,14},{7,15},{8,0},{9,1},... | collective-permute-start | bytes 884744 | tf_op jit(solution)/shard_map/ppermute | solution.py:680
  140.5 14.1 %collective-permute-start.20 = (bf16[192,768]{1,0:T(8,128)(2,1)S(1)}, bf16[192,768]{1,0:T(8,128)(2,1)S(1)}, u32[]{:S(2)}, u32[]{:S(2)}) collective-permute-start(bf16[192,768]{1,0:T(8,128)(2,1)S(1)} %get-tuple-element.311.refs_8_), channel_id=1, source_target_pairs={{0,4},{1,5},{2,3},{3,2},{4,0},{5,1},{6,7},{7,6},{8,12},{9,13},{10,... | collective-permute-start | bytes 884744 | tf_op jit(solution)/shard_map/ppermute | solution.py:680
  145.0 9.9 %collective-permute-start.21 = (bf16[384,768]{1,0:T(8,128)(2,1)S(1)}, bf16[384,768]{1,0:T(8,128)(2,1)S(1)}, u32[]{:S(2)}, u32[]{:S(2)}) collective-permute-start(bf16[384,768]{1,0:T(8,128)(2,1)S(1)} %get-tuple-element.297.refs_9_), channel_id=1, source_target_pairs={{0,1},{1,0},{2,6},{3,7},{4,5},{5,4},{6,2},{7,3},{8,9},{9,8},{10,14... | collective-permute-start | bytes 1769480 | tf_op jit(solution)/shard_map/ppermute | solution.py:680
  154.9 17.7 %collective-permute-start.28 = (bf16[384,768]{1,0:T(8,128)(2,1)S(1)}, bf16[384,768]{1,0:T(8,128)(2,1)S(1)}, u32[]{:S(2)}, u32[]{:S(2)}) collective-permute-start(bf16[384,768]{1,0:T(8,128)(2,1)S(1)} %pad_maximum_fusion.2.refs_8_.refs_9_.refs_1_), channel_id=1, source_target_pairs={{0,4},{1,5},{2,6},{3,7},{4,0},{5,1},{6,2},{7,3},{8,12},{9,13},{10,... | collective-permute-start | bytes 1769480 | tf_op jit(solution)/shard_map/ppermute | solution.py:680
  155.8 16.8 %collective-permute-start.29 = (bf16[384,768]{1,0:T(8,128)(2,1)S(1)}, bf16[384,768]{1,0:T(8,128)(2,1)S(1)}, u32[]{:S(2)}, u32[]{:S(2)}) collective-permute-start(bf16[384,768]{1,0:T(8,128)(2,1)S(1)} %pad_maximum_fusion.2.refs_8_.refs_9_.refs_1_), channel_id=1, source_target_pairs={{0,2},{1,3},{2,0},{3,1},{4,6},{5,7},{6,4},{7,5},{8,10},{9,11},{10,... | collective-permute-start | bytes 1769480 | tf_op jit(solution)/shard_map/ppermute | solution.py:680
  155.9 15.2 %collective-permute-start.30 = (bf16[96,768]{1,0:T(8,128)(2,1)S(1)}, bf16[96,768]{1,0:T(8,128)(2,1)S(1)}, u32[]{:S(2)}, u32[]{:S(2)}) collective-permute-start(bf16[96,768]{1,0:T(8,128)(2,1)S(1)} %add_convert_fusion.17.refs_10_), channel_id=1, source_target_pairs={{0,16},{1,17},{2,18},{3,19},{4,20},{5,21},{6,22},{7,23},{8,24},{9,... | collective-permute-start | bytes 442376 | tf_op jit(solution)/shard_map/ppermute | solution.py:680
  157.5 13.7 %collective-permute-start.27 = (bf16[96,768]{1,0:T(8,128)(2,1)S(1)}, bf16[96,768]{1,0:T(8,128)(2,1)S(1)}, u32[]{:S(2)}, u32[]{:S(2)}) collective-permute-start(bf16[96,768]{1,0:T(8,128)(2,1)S(1)} %get-tuple-element.319.refs_7_), channel_id=1, source_target_pairs={{0,8},{1,9},{2,10},{3,11},{4,12},{5,13},{6,14},{7,15},{8,0},{9,1},... | collective-permute-start | bytes 442376 | tf_op jit(solution)/shard_map/ppermute | solution.py:680
  161.4 11.2 %collective-permute-start.26 = (bf16[192,768]{1,0:T(8,128)(2,1)S(1)}, bf16[192,768]{1,0:T(8,128)(2,1)S(1)}, u32[]{:S(2)}, u32[]{:S(2)}) collective-permute-start(bf16[192,768]{1,0:T(8,128)(2,1)S(1)} %get-tuple-element.309.refs_6_), channel_id=1, source_target_pairs={{0,4},{1,5},{2,3},{3,2},{4,0},{5,1},{6,7},{7,6},{8,12},{9,13},{10,... | collective-permute-start | bytes 884744 | tf_op jit(solution)/shard_map/ppermute | solution.py:680
  172.6 4.9 %collective-permute-start.37 = (f32[8448]{0:T(1024)S(1)}, f32[8448]{0:T(1024)S(1)}, u32[]{:S(2)}, u32[]{:S(2)}) collective-permute-start(f32[8448]{0:T(1024)S(1)} %pad_maximum_fusion.9), channel_id=1, source_target_pairs={{0,1},{1,0},{2,3},{3,2},{4,5},{5,4},{6,7},{7,6},{8,9},{9,8},{10,11... | collective-permute-start | bytes 101384 | tf_op jit(solution)/shard_map/ppermute | solution.py:680
  173.2 17.7 %collective-permute-start.35 = (bf16[384,768]{1,0:T(8,128)(2,1)S(1)}, bf16[384,768]{1,0:T(8,128)(2,1)S(1)}, u32[]{:S(2)}, u32[]{:S(2)}) collective-permute-start(bf16[384,768]{1,0:T(8,128)(2,1)S(1)} %collective-permute-done.28.refs_2_), channel_id=1, source_target_pairs={{0,2},{1,3},{2,0},{3,1},{4,6},{5,7},{6,4},{7,5},{8,10},{9,11},{10,... | collective-permute-start | bytes 1769480 | tf_op jit(solution)/shard_map/ppermute | solution.py:680
  173.3 17.6 %collective-permute-start.36 = (bf16[192,768]{1,0:T(8,128)(2,1)S(1)}, bf16[192,768]{1,0:T(8,128)(2,1)S(1)}, u32[]{:S(2)}, u32[]{:S(2)}) collective-permute-start(bf16[192,768]{1,0:T(8,128)(2,1)S(1)} %pad_maximum_fusion.6), channel_id=1, source_target_pairs={{0,8},{1,9},{2,10},{3,11},{4,12},{5,13},{6,14},{7,15},{8,0},{9,1},... | collective-permute-start | bytes 884744 | tf_op jit(solution)/shard_map/ppermute | solution.py:680
  173.8 8.9 %collective-permute-start.34 = (bf16[48,768]{1,0:T(8,128)(2,1)S(1)}, bf16[48,768]{1,0:T(8,128)(2,1)S(1)}, u32[]{:S(2)}, u32[]{:S(2)}) collective-permute-start(bf16[48,768]{1,0:T(8,128)(2,1)S(1)} %add_convert_fusion.32), channel_id=1, source_target_pairs={{0,16},{1,17},{2,18},{3,19},{4,20},{5,21},{6,22},{7,23},{8,24},{9,... | collective-permute-start | bytes 221192 | tf_op jit(solution)/shard_map/ppermute | solution.py:680
  177.5 8.4 %collective-permute-start.31 = (bf16[48,768]{1,0:T(8,128)(2,1)S(1)}, bf16[48,768]{1,0:T(8,128)(2,1)S(1)}, u32[]{:S(2)}, u32[]{:S(2)}) collective-permute-start(bf16[48,768]{1,0:T(8,128)(2,1)S(1)} %get-tuple-element.322), channel_id=1, source_target_pairs={{0,16},{1,17},{2,18},{3,19},{4,20},{5,21},{6,22},{7,23},{8,24},{9,... | collective-permute-start | bytes 221192 | tf_op jit(solution)/shard_map/ppermute | solution.py:680
  177.6 9.9 %collective-permute-start.32 = (bf16[48,768]{1,0:T(8,128)(2,1)S(1)}, bf16[48,768]{1,0:T(8,128)(2,1)S(1)}, u32[]{:S(2)}, u32[]{:S(2)}) collective-permute-start(bf16[48,768]{1,0:T(8,128)(2,1)S(1)} %get-tuple-element.321), channel_id=1, source_target_pairs={{0,8},{1,9},{2,10},{3,11},{4,12},{5,13},{6,14},{7,15},{8,0},{9,1},... | collective-permute-start | bytes 221192 | tf_op jit(solution)/shard_map/ppermute | solution.py:680
  182.7 8.2 %collective-permute-start.33 = (bf16[48,768]{1,0:T(8,128)(2,1)S(1)}, bf16[48,768]{1,0:T(8,128)(2,1)S(1)}, u32[]{:S(2)}, u32[]{:S(2)}) collective-permute-start(bf16[48,768]{1,0:T(8,128)(2,1)S(1)} %get-tuple-element.320), channel_id=1, source_target_pairs={{0,24},{1,25},{2,26},{3,27},{4,28},{5,29},{6,30},{7,31},{8,16},{9,... | collective-permute-start | bytes 221192 | tf_op jit(solution)/shard_map/ppermute | solution.py:680
  191.0 15.2 %collective-permute-start.41 = (bf16[384,768]{1,0:T(8,128)(2,1)S(1)}, bf16[384,768]{1,0:T(8,128)(2,1)S(1)}, u32[]{:S(2)}, u32[]{:S(2)}) collective-permute-start(bf16[384,768]{1,0:T(8,128)(2,1)S(1)} %pad_maximum_fusion.3.refs_8_.refs_9_.refs_1_), channel_id=1, source_target_pairs={{0,4},{1,5},{2,6},{3,7},{4,0},{5,1},{6,2},{7,3},{8,12},{9,13},{10,... | collective-permute-start | bytes 1769480 | tf_op jit(solution)/shard_map/ppermute | solution.py:680
  191.5 14.7 %collective-permute-start.42 = (bf16[384,768]{1,0:T(8,128)(2,1)S(1)}, bf16[384,768]{1,0:T(8,128)(2,1)S(1)}, u32[]{:S(2)}, u32[]{:S(2)}) collective-permute-start(bf16[384,768]{1,0:T(8,128)(2,1)S(1)} %pad_maximum_fusion.3.refs_8_.refs_9_.refs_1_), channel_id=1, source_target_pairs={{0,2},{1,3},{2,0},{3,1},{4,6},{5,7},{6,4},{7,5},{8,10},{9,11},{10,... | collective-permute-start | bytes 1769480 | tf_op jit(solution)/shard_map/ppermute | solution.py:680
  192.2 11.6 %collective-permute-start.38 = (bf16[48,1536]{1,0:T(8,128)(2,1)S(1)}, bf16[48,1536]{1,0:T(8,128)(2,1)S(1)}, u32[]{:S(2)}, u32[]{:S(2)}) collective-permute-start(bf16[48,1536]{1,0:T(8,128)(2,1)S(1)} %get-tuple-element.324.refs_5_.refs_6_.refs_7_), channel_id=1, source_target_pairs={{0,16},{1,17},{2,18},{3,19},{4,20},{5,21},{6,22},{7,23},{8,24},{9,... | collective-permute-start | bytes 442376 | tf_op jit(solution)/shard_map/ppermute | solution.py:680
  193.2 10.6 %collective-permute-start.39 = (bf16[48,1536]{1,0:T(8,128)(2,1)S(1)}, bf16[48,1536]{1,0:T(8,128)(2,1)S(1)}, u32[]{:S(2)}, u32[]{:S(2)}) collective-permute-start(bf16[48,1536]{1,0:T(8,128)(2,1)S(1)} %get-tuple-element.324.refs_5_.refs_6_.refs_7_), channel_id=1, source_target_pairs={{0,8},{1,9},{2,10},{3,11},{4,12},{5,13},{6,14},{7,15},{8,0},{9,1},... | collective-permute-start | bytes 442376 | tf_op jit(solution)/shard_map/ppermute | solution.py:680
  194.5 11.6 %collective-permute-start.40 = (bf16[48,1536]{1,0:T(8,128)(2,1)S(1)}, bf16[48,1536]{1,0:T(8,128)(2,1)S(1)}, u32[]{:S(2)}, u32[]{:S(2)}) collective-permute-start(bf16[48,1536]{1,0:T(8,128)(2,1)S(1)} %get-tuple-element.324.refs_5_.refs_6_.refs_7_), channel_id=1, source_target_pairs={{0,24},{1,25},{2,26},{3,27},{4,28},{5,29},{6,30},{7,31},{8,16},{9,... | collective-permute-start | bytes 442376 | tf_op jit(solution)/shard_map/ppermute | solution.py:680
  206.2 4.0 %collective-permute-start.46 = (f32[8448]{0:T(1024)S(1)}, f32[8448]{0:T(1024)S(1)}, u32[]{:S(2)}, u32[]{:S(2)}) collective-permute-start(f32[8448]{0:T(1024)S(1)} %fusion), channel_id=1, source_target_pairs={{0,4},{1,5},{2,6},{3,7},{4,0},{5,1},{6,2},{7,3},{8,12},{9,13},{10,... | collective-permute-start | bytes 101384 | tf_op jit(solution)/shard_map/ppermute | solution.py:680
  207.8 9.9 %collective-permute-start.44 = (bf16[192,1536]{1,0:T(8,128)(2,1)S(1)}, bf16[192,1536]{1,0:T(8,128)(2,1)S(1)}, u32[]{:S(2)}, u32[]{:S(2)}) collective-permute-start(bf16[192,1536]{1,0:T(8,128)(2,1)S(1)} %pad_maximum_fusion.4), channel_id=1, source_target_pairs={{0,4},{1,5},{2,3},{3,2},{4,0},{5,1},{6,7},{7,6},{8,12},{9,13},{10,... | collective-permute-start | bytes 1769480 | tf_op jit(solution)/shard_map/ppermute | solution.py:680
  208.4 9.4 %collective-permute-start.45 = (bf16[384,768]{1,0:T(8,128)(2,1)S(1)}, bf16[384,768]{1,0:T(8,128)(2,1)S(1)}, u32[]{:S(2)}, u32[]{:S(2)}) collective-permute-start(bf16[384,768]{1,0:T(8,128)(2,1)S(1)} %collective-permute-done.41.refs_2_), channel_id=1, source_target_pairs={{0,2},{1,3},{2,0},{3,1},{4,6},{5,7},{6,4},{7,5},{8,10},{9,11},{10,... | collective-permute-start | bytes 1769480 | tf_op jit(solution)/shard_map/ppermute | solution.py:680
  217.8 16.3 %collective-permute-start.47 = (bf16[384,1536]{1,0:T(8,128)(2,1)S(1)}, bf16[384,1536]{1,0:T(8,128)(2,1)S(1)}, u32[]{:S(2)}, u32[]{:S(2)}) collective-permute-start(bf16[384,1536]{1,0:T(8,128)(2,1)S(1)} %constant_dynamic-update-slice_fusion.refs_7_.refs_8_.refs_1_), channel_id=1, source_target_pairs={{0,1},{1,0},{2,6},{3,7},{4,5},{5,4},{6,2},{7,3},{8,9},{9,8},{10,14... | collective-permute-start | bytes 3538952 | tf_op jit(solution)/shard_map/ppermute | solution.py:680
  219.4 14.7 %collective-permute-start.48 = (bf16[384,1536]{1,0:T(8,128)(2,1)S(1)}, bf16[384,1536]{1,0:T(8,128)(2,1)S(1)}, u32[]{:S(2)}, u32[]{:S(2)}) collective-permute-start(bf16[384,1536]{1,0:T(8,128)(2,1)S(1)} %constant_dynamic-update-slice_fusion.refs_7_.refs_8_.refs_1_), channel_id=1, source_target_pairs={{0,2},{1,3},{2,0},{3,1},{4,6},{5,7},{6,4},{7,5},{8,10},{9,11},{10,... | collective-permute-start | bytes 3538952 | tf_op jit(solution)/shard_map/ppermute | solution.py:680
  219.4 10.0 %collective-permute-start.49 = (f32[8448]{0:T(1024)S(1)}, f32[8448]{0:T(1024)S(1)}, u32[]{:S(2)}, u32[]{:S(2)}) collective-permute-start(f32[8448]{0:T(1024)S(1)} %add.278.refs_9_.refs_10_.refs_11_), channel_id=1, source_target_pairs={{0,16},{1,17},{2,18},{3,19},{4,20},{5,21},{6,22},{7,23},{8,24},{9,... | collective-permute-start | bytes 101384 | tf_op jit(solution)/shard_map/ppermute | solution.py:680
  222.3 7.2 %collective-permute-start.50 = (f32[8448]{0:T(1024)S(1)}, f32[8448]{0:T(1024)S(1)}, u32[]{:S(2)}, u32[]{:S(2)}) collective-permute-start(f32[8448]{0:T(1024)S(1)} %add.278.refs_9_.refs_10_.refs_11_), channel_id=1, source_target_pairs={{0,8},{1,9},{2,10},{3,11},{4,12},{5,13},{6,14},{7,15},{8,0},{9,1},... | collective-permute-start | bytes 101384 | tf_op jit(solution)/shard_map/ppermute | solution.py:680
  222.4 7.1 %collective-permute-start.51 = (f32[8448]{0:T(1024)S(1)}, f32[8448]{0:T(1024)S(1)}, u32[]{:S(2)}, u32[]{:S(2)}) collective-permute-start(f32[8448]{0:T(1024)S(1)} %add.278.refs_9_.refs_10_.refs_11_), channel_id=1, source_target_pairs={{0,24},{1,25},{2,26},{3,27},{4,28},{5,29},{6,30},{7,31},{8,16},{9,... | collective-permute-start | bytes 101384 | tf_op jit(solution)/shard_map/ppermute | solution.py:680
  (42 other events, 178.2 us)
where the time goes:
time: 248 us; the launch traced here: 246 us
  Pallas kernels  124 us (50%)
  starting transfers between devices  58 us (23%)
  waiting for transfers between devices  46.2 us (19%)
  local copies, waits for them, and re-layouts  9.43 us (4%)
  other arithmetic  5.13 us (2%)
  between operations  3.27 us (1%)
    pallas_call x11, Pallas kernels, call(): pl.pallas_call(body, out_shape=tuple((o for _, o in outs)), in_specs=[spe...  124 us
    ppermute x53, starting transfers between devices, swap(): return lax.ppermute(value, ('batch', 'tp'), pairs)  58 us
    ppermute x53, waiting for transfers between devices, swap(): return lax.ppermute(value, ('batch', 'tp'), pairs)  46.2 us
    unnamed x77, local copies, waits for them, and re-layouts  6.14 us
  transfers between devices with their start and end apart: 53, of which 17 were waited for; matrix products, arithmetic and copies ran while one was open for 3% of the time, Pallas kernels for 48%

commit v1 on v0

--- a/solution.py
+++ b/solution.py
@@ -18,7 +18,7 @@
 S = jax.ShapeDtypeStruct
 TIMES = {"attend_fwd": 24, "ffn_chunk": 17, "layer_end": 9, "mid": 8, "value_bwd": 13, "query_bwd": 13, "input_back": 10, "finish_ffn": 5, "finish_pair": 5}
 MIB = 2**20
-GRANT = 52
+GRANT = 48
 
 
 def dot(a, b):

time: 248 us -> 246 us (level)
  Pallas kernels: 124 us -> 117 us
  waiting for transfers between devices: 46.2 us -> 52.8 us
    pallas_call x11, Pallas kernels: 124 us -> 117 us  [call(): pl.pallas_call(body, out_shape=tuple((o for _, o in outs)), in_specs=[spe...]
    ppermute x53, waiting for transfers between devices: 46.2 us -> 52.8 us  [swap(): return lax.ppermute(value, ('batch', 'tp'), pairs)]
    unnamed x77 -> x73, local copies, waits for them, and re-layouts: 6.14 us -> 4.33 us
  transfers between devices with their start and end apart: 53 -> 53, of which waited for: 17 -> 16; matrix products, arithmetic and copies ran while one was open for 3% -> 3% of each run, Pallas kernels for 48% -> 46%
where the time goes in v1:
time: 246 us; the launch traced here: 243 us
  Pallas kernels  117 us (48%)
  starting transfers between devices  56 us (23%)
  waiting for transfers between devices  52.8 us (21%)
  local copies, waits for them, and re-layouts  8.37 us (3%)
  other arithmetic  5.94 us (2%)
  between operations  3.28 us (1%)
    pallas_call x11, Pallas kernels, call(): pl.pallas_call(body, out_shape=tuple((o for _, o in outs)), in_specs=[spe...  117 us
    ppermute x53, starting transfers between devices, swap(): return lax.ppermute(value, ('batch', 'tp'), pairs)  56 us
    ppermute x53, waiting for transfers between devices, swap(): return lax.ppermute(value, ('batch', 'tp'), pairs)  52.8 us
  transfers between devices with their start and end apart: 53, of which 16 were waited for; matrix products, arithmetic and copies ran while one was open for 3% of the time, Pallas kernels for 46%

profile of v1, /device:TPU:0, one launch (start us, length us, event | category | flops | bytes accessed | tf_op | source)
XLA Modules:
  0.0 243.0 jit_solution(15784140860319444236)
XLA Ops:
  0.7 2.6 %constant_dynamic-slice_fusion = (bf16[384,768]{1,0:T(8,128)(2,1)S(1)}, bf16[384,768]{1,0:T(8,128)(2,1)S(1)}, bf16[384,768]{1,0:T(8,128)(2,1)S(1)}, bf16[384,768]{1,0:T(8,128)(2,1)}) fusion(bf16[1536,768]{1,0:T(8,128)(2,1)} %refs_6_.5, s32[]{:T(128)S(6)} %select_n.96, s32[]{:T(128)S(6)} %select_n.95, bf16[768,1536]{1,0:T(8,128)(2,1)} %refs_5_.6, s32[]{:T(128)S(6)} %select_n.94), kind=kLoop, calls=%fused_computation.59 | loop fusion | bytes 4718604 | tf_op jit(solution)/shard_map/dynamic_slice | solution.py:852
  4.5 3.0 %collective-permute-start = (bf16[768,768]{1,0:T(8,128)(2,1)}, bf16[768,768]{1,0:T(8,128)(2,1)}, u32[]{:S(2)}, u32[]{:S(2)}) collective-permute-start(bf16[768,768]{1,0:T(8,128)(2,1)} %pad_maximum_fusion), channel_id=1, source_target_pairs={{0,1},{1,0},{2,3},{3,2},{4,5},{5,4},{6,7},{7,6},{8,9},{9,8},{10,11... | collective-permute-start | bytes 3538952 | tf_op jit(solution)/shard_map/ppermute | solution.py:680
  9.2 22.9 %attend_fwd.1 = (bf16[3,768,768]{2,1,0:T(8,128)(2,1)}, bf16[2,768,384]{2,1,0:T(8,128)(2,1)S(1)}, bf16[6,3,128,512]{3,2,1,0:T(8,128)(2,1)}, bf16[2,768,768]{2,1,0...) custom-call(s32[6]{0:T(128)S(1)} %stack.27.refs_0_, ...), custom_call_target="tpu_custom_call" | custom-call | flops 27599998976 | bytes 16777216 | tf_op jit(solution)/shard_map/attend_fwd/pallas_call | solution.py:94
  33.9 1.8 collective-permute-start.2
  37.9 17.3 %ffn_chunk.2 = (bf16[768,768]{1,0:T(8,128)(2,1)S(1)}, bf16[768,768]{1,0:T(8,128)(2,1)S(1)}, bf16[1536,768]{1,0:T(8,128)(2,1)}, bf16[2,768,768]{2,1,0:T(8,128)(2,...) custom-call(s32[6]{0:T(128)S(1)} %stack.27.refs_0_, ...), custom_call_target="tpu_custom_call" | custom-call | flops 19549999104 | bytes 12582912 | tf_op jit(solution)/shard_map/ffn_chunk/pallas_call | solution.py:94
  55.4 7.0 %collective-permute-done.2.refs_7_ = bf16[768,768]{1,0:T(8,128)(2,1)S(1)} collective-permute-done((bf16[768,768]{1,0:T(8,128)(2,1)S(1)}, bf16[768,768]{1,0:T(8,128)(2,1)S(1)}, u32[]{:S(2)}, u32[]{:S(2)}) %collective-permute-start.2) | collective-permute-done | bytes 1179680 | tf_op jit(solution)/shard_map/ppermute | solution.py:680
  62.9 1.6 add_convert_fusion.3.refs_11_
  64.5 1.8 collective-permute-start.6
  67.3 16.9 %ffn_chunk.3 = (bf16[768,768]{1,0:T(8,128)(2,1)S(1)}, bf16[768,768]{1,0:T(8,128)(2,1)S(1)}, bf16[1536,768]{1,0:T(8,128)(2,1)}, bf16[2,768,768]{2,1,0:T(8,128)(2,...) custom-call(s32[6]{0:T(128)S(1)} %stack.27.refs_0_, ...), custom_call_target="tpu_custom_call" | custom-call | flops 19549999104 | bytes 12582912 | tf_op jit(solution)/shard_map/ffn_chunk/pallas_call | solution.py:94
  84.9 1.5 collective-permute-start.9
  88.4 5.2 %mid.1 = (f32[768,768]{1,0:T(8,128)}, bf16[768,768]{1,0:T(8,128)(2,1)S(1)}, bf16[768,768]{1,0:T(8,128)(2,1)S(1)}, f32[4,768]{1,0:T(4,128)S(1)}) custom-call(f32[768,768]{1,0:T(8,128)} %get-tuple-element.180.refs_0_, bf16[768,768]{1,0:T(8,128)(2,1)S(1)} %copy-done, f32[768,768]{1,0:T(8,128)} %get-tuple-element.234.refs_2_.refs_0_, ...), custom_call_target="tpu_custom_call" | custom-call | flops 9200000000 | bytes 8388608 | tf_op jit(solution)/shard_map/mid/pallas_call | solution.py:94
  94.7 4.8 %collective-permute-done.9 = bf16[384,768]{1,0:T(8,128)(2,1)S(1)} collective-permute-done((bf16[384,768]{1,0:T(8,128)(2,1)S(1)}, bf16[384,768]{1,0:T(8,128)(2,1)S(1)}, u32[]{:S(2)}, u32[]{:S(2)}) %collective-permute-start.9) | collective-permute-done | bytes 589856 | tf_op jit(solution)/shard_map/ppermute | solution.py:680
  99.6 2.7 %collective-permute-start.10 = (bf16[96,768]{1,0:T(8,128)(2,1)S(1)}, bf16[96,768]{1,0:T(8,128)(2,1)S(1)}, u32[]{:S(2)}, u32[]{:S(2)}) collective-permute-start(bf16[96,768]{1,0:T(8,128)(2,1)S(1)} %get-tuple-element.317.refs_6_), channel_id=1, source_target_pairs={{0,16},{1,17},{2,18},{3,19},{4,20},{5,21},{6,22},{7,23},{8,24},{9,... | collective-permute-start | bytes 442376 | tf_op jit(solution)/shard_map/ppermute | solution.py:680
  102.3 1.6 collective-permute-start.11
  104.1 12.3 %value_bwd.1 = (bf16[768,768]{1,0:T(8,128)(2,1)S(1)}, bf16[768,768]{1,0:T(8,128)(2,1)S(1)}, bf16[768,768]{1,0:T(8,128)(2,1)S(1)}, bf16[768,1536]{1,0:T(8,128)(2,...) custom-call(s32[6]{0:T(128)S(1)} %stack.27.refs_0_, bf16[768,768]{1,0:T(8,128)(2,1)S(1)} %get-tuple-element.193.refs_1_, ...), custom_call_target="tpu_custom_call" | custom-call | flops 14949999616 | bytes 8388608 | tf_op jit(solution)/shard_map/value_bwd/pallas_call | solution.py:94
  117.0 1.5 collective-permute-start.18
  118.7 1.8 collective-permute-start.17
  121.8 12.6 %query_bwd.1 = (bf16[768,768]{1,0:T(8,128)(2,1)S(1)}, bf16[768,768]{1,0:T(8,128)(2,1)S(1)}, bf16[2,768,768]{2,1,0:T(8,128)(2,1)}, f32[2,768]{1,0:T(2,128)S(1)}) custom-call(s32[6]{0:T(128)S(1)} %stack.27.refs_0_, bf16[768,1536]{1,0:T(8,128)(2,1)} %get-tuple-element.207.refs_1_, bf16[6,3,128,512]{3,2,1,0:T(8,128)(2,1)} %get-tuple-element.208.refs_2_, ...), custom_call_target="tpu_custom_call" | custom-call | flops 14949999616 | bytes 12582912 | tf_op jit(solution)/shard_map/query_bwd/pallas_call | solution.py:94
  134.6 1.3 collective-permute-start.23
  135.9 2.2 collective-permute-start.24
  138.1 1.4 collective-permute-start.25
  139.5 1.2 collective-permute-start.22
  142.2 3.2 %collective-permute-done.23 = bf16[96,768]{1,0:T(8,128)(2,1)S(1)} collective-permute-done((bf16[96,768]{1,0:T(8,128)(2,1)S(1)}, bf16[96,768]{1,0:T(8,128)(2,1)S(1)}, u32[]{:S(2)}, u32[]{:S(2)}) %collective-permute-start.23) | collective-permute-done | bytes 147488 | tf_op jit(solution)/shard_map/ppermute | solution.py:680
  146.6 8.8 %input_back.1 = (bf16[768,768]{1,0:T(8,128)(2,1)}, f32[2,768]{1,0:T(2,128)S(1)}) custom-call(bf16[2,768,768]{2,1,0:T(8,128)(2,1)} %get-tuple-element.224.refs_0_, bf16[768,768]{1,0:T(8,128)(2,1)S(1)} %get-tuple-element.225.refs_1_, bf16[768,768]{1,0:T(8,128)(2,1)S(1)} %copy-done.3, bf16[768,768]{1,0:T(8,128)(2,1)S(1)} %copy-done.4, ...), custom_call_target="tpu_custom_call" | custom-call | flops 11500000256 | bytes 8388608 | tf_op jit(solution)/shard_map/input_back/pallas_call | solution.py:94
  156.4 1.8 collective-permute-start.30
  158.3 1.7 collective-permute-start.27
  161.3 8.3 %layer_end.1 = bf16[768,768]{1,0:T(8,128)(2,1)} custom-call(f32[768,768]{1,0:T(8,128)S(1)} %copy-done.21, f32[768]{0:T(1024)S(1)} %copy-done.15, bf16[2,768,768]{2,1,0:T(8,128)(2,1)S(1)} %copy-done.22, bf16[2,768,768]{2,1,0:T(8,128)(2,1)} %get-tuple-element.236.refs_3_, bf16[2,768,768]{2,1,0:T(8,128)(2,1)} %get-tuple-element.237.refs_4_, ...), custom_call_target="tpu_custom_call" | custom-call | flops 10350000128 | bytes 12582912 | tf_op jit(solution)/shard_map/layer_end/pallas_call | solution.py:94
  169.5 3.5 %collective-permute-done.26 = bf16[192,768]{1,0:T(8,128)(2,1)S(1)} collective-permute-done((bf16[192,768]{1,0:T(8,128)(2,1)S(1)}, bf16[192,768]{1,0:T(8,128)(2,1)S(1)}, u32[]{:S(2)}, u32[]{:S(2)}) %collective-permute-start.26) | collective-permute-done | bytes 294944 | tf_op jit(solution)/shard_map/ppermute | solution.py:680
  173.1 1.2 collective-permute-start.37
  174.9 3.1 %collective-permute-start.34 = (bf16[48,768]{1,0:T(8,128)(2,1)S(1)}, bf16[48,768]{1,0:T(8,128)(2,1)S(1)}, u32[]{:S(2)}, u32[]{:S(2)}) collective-permute-start(bf16[48,768]{1,0:T(8,128)(2,1)S(1)} %add_convert_fusion.32), channel_id=1, source_target_pairs={{0,16},{1,17},{2,18},{3,19},{4,20},{5,21},{6,22},{7,23},{8,24},{9,... | collective-permute-start | bytes 221192 | tf_op jit(solution)/shard_map/ppermute | solution.py:680
  178.1 1.4 collective-permute-start.32
  179.5 4.2 %collective-permute-done.34 = bf16[48,768]{1,0:T(8,128)(2,1)S(1)} collective-permute-done((bf16[48,768]{1,0:T(8,128)(2,1)S(1)}, bf16[48,768]{1,0:T(8,128)(2,1)S(1)}, u32[]{:S(2)}, u32[]{:S(2)}) %collective-permute-start.34) | collective-permute-done | bytes 73760 | tf_op jit(solution)/shard_map/ppermute | solution.py:680
  183.7 3.2 %collective-permute-start.33 = (bf16[48,768]{1,0:T(8,128)(2,1)S(1)}, bf16[48,768]{1,0:T(8,128)(2,1)S(1)}, u32[]{:S(2)}, u32[]{:S(2)}) collective-permute-start(bf16[48,768]{1,0:T(8,128)(2,1)S(1)} %get-tuple-element.320), channel_id=1, source_target_pairs={{0,24},{1,25},{2,26},{3,27},{4,28},{5,29},{6,30},{7,31},{8,16},{9,... | collective-permute-start | bytes 221192 | tf_op jit(solution)/shard_map/ppermute | solution.py:680
  187.0 1.6 collective-permute-done.32
  188.5 3.3 %collective-permute-done.33 = bf16[48,768]{1,0:T(8,128)(2,1)S(1)} collective-permute-done((bf16[48,768]{1,0:T(8,128)(2,1)S(1)}, bf16[48,768]{1,0:T(8,128)(2,1)S(1)}, u32[]{:S(2)}, u32[]{:S(2)}) %collective-permute-start.33) | collective-permute-done | bytes 73760 | tf_op jit(solution)/shard_map/ppermute | solution.py:680
  195.3 2.4 %collective-permute-start.40 = (bf16[48,1536]{1,0:T(8,128)(2,1)S(1)}, bf16[48,1536]{1,0:T(8,128)(2,1)S(1)}, u32[]{:S(2)}, u32[]{:S(2)}) collective-permute-start(bf16[48,1536]{1,0:T(8,128)(2,1)S(1)} %get-tuple-element.324.refs_5_.refs_6_.refs_7_), channel_id=1, source_target_pairs={{0,24},{1,25},{2,26},{3,27},{4,28},{5,29},{6,30},{7,31},{8,16},{9,... | collective-permute-start | bytes 442376 | tf_op jit(solution)/shard_map/ppermute | solution.py:680
  197.7 3.8 %finish_ffn.2 = (f32[768,1536]{1,0:T(8,128)}, f32[1536,768]{1,0:T(8,128)}) custom-call(s32[6]{0:T(128)S(1)} %stack.27.refs_0_, bf16[384,768]{1,0:T(8,128)(2,1)S(1)} %pad_maximum_fusion.2.refs_8_.refs_9_.refs_1_, bf16[384,768]{1,0:T(8,128)(2,1)S(1)} %collective-permute-done.28.refs_2_, bf16[384,768]{1,0:T(8,128)(2,1)S(1)} %collective-permute-done.29.refs_3_, ...), custom_call_target="tpu_custom_call" | custom-call | flops 5750000128 | bytes 4194304 | tf_op jit(solution)/shard_map/finish_ffn/pallas_call | solution.py:94
  201.5 3.4 %collective-permute-done.38 = bf16[48,1536]{1,0:T(8,128)(2,1)S(1)} collective-permute-done((bf16[48,1536]{1,0:T(8,128)(2,1)S(1)}, bf16[48,1536]{1,0:T(8,128)(2,1)S(1)}, u32[]{:S(2)}, u32[]{:S(2)}) %collective-permute-start.38) | collective-permute-done | bytes 147488 | tf_op jit(solution)/shard_map/ppermute | solution.py:680
  204.9 2.3 collective-permute-done.40
  207.2 1.6 collective-permute-start.46
  209.4 1.8 collective-permute-done.46
  211.2 7.5 %collective-permute-done.44 = bf16[192,1536]{1,0:T(8,128)(2,1)S(1)} collective-permute-done((bf16[192,1536]{1,0:T(8,128)(2,1)S(1)}, bf16[192,1536]{1,0:T(8,128)(2,1)S(1)}, u32[]{:S(2)}, u32[]{:S(2)}) %collective-permute-start.44) | collective-permute-done | bytes 589856 | tf_op jit(solution)/shard_map/ppermute | solution.py:680
  219.7 2.9 %collective-permute-start.49 = (f32[8448]{0:T(1024)S(1)}, f32[8448]{0:T(1024)S(1)}, u32[]{:S(2)}, u32[]{:S(2)}) collective-permute-start(f32[8448]{0:T(1024)S(1)} %add.278.refs_9_.refs_10_.refs_11_), channel_id=1, source_target_pairs={{0,16},{1,17},{2,18},{3,19},{4,20},{5,21},{6,22},{7,23},{8,24},{9,... | collective-permute-start | bytes 101384 | tf_op jit(solution)/shard_map/ppermute | solution.py:680
  222.7 2.3 collective-permute-start.51
  225.0 3.8 %finish_ffn.3 = (f32[768,1536]{1,0:T(8,128)}, f32[1536,768]{1,0:T(8,128)}) custom-call(s32[6]{0:T(128)S(1)} %stack.27.refs_0_, bf16[384,768]{1,0:T(8,128)(2,1)S(1)} %pad_maximum_fusion.3.refs_8_.refs_9_.refs_1_, bf16[384,768]{1,0:T(8,128)(2,1)S(1)} %collective-permute-done.41.refs_2_, ...), custom_call_target="tpu_custom_call", output_to_operand_aliasing={{0}: (5, {}), {1}: (6, {})} | custom-call | flops 5750000128 | bytes 4194304 | tf_op jit(solution)/shard_map/finish_ffn/pallas_call | solution.py:94
  228.9 6.2 %collective-permute-done.47.refs_2_ = bf16[384,1536]{1,0:T(8,128)(2,1)S(1)} collective-permute-done((bf16[384,1536]{1,0:T(8,128)(2,1)S(1)}, bf16[384,1536]{1,0:T(8,128)(2,1)S(1)}, u32[]{:S(2)}, u32[]{:S(2)}) %collective-permute-start.47) | collective-permute-done | bytes 1179680 | tf_op jit(solution)/shard_map/ppermute | solution.py:680
  236.3 1.6 collective-permute-done.52.refs_4_
  237.9 4.8 %finish_pair.1 = (f32[768,768]{1,0:T(8,128)}, f32[768,768]{1,0:T(8,128)}, f32[768,768]{1,0:T(8,128)}, f32[768,768]{1,0:T(8,128)}) custom-call(s32[6]{0:T(128)S(1)} %stack.27.refs_0_, bf16[384,1536]{1,0:T(8,128)(2,1)S(1)} %constant_dynamic-update-slice_fusion.refs_7_.refs_8_.refs_1_, bf16[384,1536]{1,0:T(8,128)(2,1)S(1)} %collective-permute-done.47.refs_2_, ...), custom_call_target="tpu_custom_call" | custom-call | flops 5750000128 | bytes 8388608 | tf_op jit(solution)/shard_map/finish_pair/pallas_call | solution.py:94
  (187 shorter events, 25.4 us)
Async XLA Ops:
  4.5 29.3 %collective-permute-start = (bf16[768,768]{1,0:T(8,128)(2,1)}, bf16[768,768]{1,0:T(8,128)(2,1)}, u32[]{:S(2)}, u32[]{:S(2)}) collective-permute-start(bf16[768,768]{1,0:T(8,128)(2,1)} %pad_maximum_fusion), channel_id=1, source_target_pairs={{0,1},{1,0},{2,3},{3,2},{4,5},{5,4},{6,7},{7,6},{8,9},{9,8},{10,11... | collective-permute-start | bytes 3538952 | tf_op jit(solution)/shard_map/ppermute | solution.py:680
  7.5 26.3 %collective-permute-start.1 = (bf16[1536]{0:T(1024)(128)(2,1)S(1)}, bf16[1536]{0:T(1024)(128)(2,1)S(1)}, u32[]{:S(2)}, u32[]{:S(2)}) collective-permute-start(bf16[1536]{0:T(1024)(128)(2,1)S(1)} %copy-done.32), channel_id=1, source_target_pairs={{0,1},{1,0},{2,3},{3,2},{4,5},{5,4},{6,7},{7,6},{8,9},{9,8},{10,11... | collective-permute-start | bytes 9224 | tf_op jit(solution)/shard_map/ppermute | solution.py:680
  33.9 28.4 %collective-permute-start.2 = (bf16[768,768]{1,0:T(8,128)(2,1)S(1)}, bf16[768,768]{1,0:T(8,128)(2,1)S(1)}, u32[]{:S(2)}, u32[]{:S(2)}) collective-permute-start(bf16[768,768]{1,0:T(8,128)(2,1)S(1)} %pad_maximum_fusion.1), channel_id=1, source_target_pairs={{0,1},{1,0},{2,3},{3,2},{4,5},{5,4},{6,7},{7,6},{8,9},{9,8},{10,11... | collective-permute-start | bytes 3538952 | tf_op jit(solution)/shard_map/ppermute | solution.py:680
  55.2 7.2 %collective-permute-start.4 = (bf16[768,768]{1,0:T(8,128)(2,1)S(1)}, bf16[768,768]{1,0:T(8,128)(2,1)S(1)}, u32[]{:S(2)}, u32[]{:S(2)}) collective-permute-start(bf16[768,768]{1,0:T(8,128)(2,1)S(1)} %get-tuple-element.167), channel_id=1, source_target_pairs={{0,2},{1,3},{2,0},{3,1},{4,6},{5,7},{6,4},{7,5},{8,10},{9,11},{10,... | collective-permute-start | bytes 3538952 | tf_op jit(solution)/shard_map/ppermute | solution.py:680
  62.4 21.8 %collective-permute-start.7 = (bf16[768,768]{1,0:T(8,128)(2,1)S(1)}, bf16[768,768]{1,0:T(8,128)(2,1)S(1)}, u32[]{:S(2)}, u32[]{:S(2)}) collective-permute-start(bf16[768,768]{1,0:T(8,128)(2,1)S(1)} %get-tuple-element.172.refs_12_), channel_id=1, source_target_pairs={{0,2},{1,3},{2,0},{3,1},{4,6},{5,7},{6,4},{7,5},{8,10},{9,11},{10,... | collective-permute-start | bytes 3538952 | tf_op jit(solution)/shard_map/ppermute | solution.py:680
  64.5 19.8 %collective-permute-start.6 = (bf16[768,768]{1,0:T(8,128)(2,1)S(1)}, bf16[768,768]{1,0:T(8,128)(2,1)S(1)}, u32[]{:S(2)}, u32[]{:S(2)}) collective-permute-start(bf16[768,768]{1,0:T(8,128)(2,1)S(1)} %add_convert_fusion.3.refs_11_), channel_id=1, source_target_pairs={{0,1},{1,0},{2,6},{3,7},{4,5},{5,4},{6,2},{7,3},{8,9},{9,8},{10,14... | collective-permute-start | bytes 3538952 | tf_op jit(solution)/shard_map/ppermute | solution.py:680
  84.9 14.5 %collective-permute-start.9 = (bf16[384,768]{1,0:T(8,128)(2,1)S(1)}, bf16[384,768]{1,0:T(8,128)(2,1)S(1)}, u32[]{:S(2)}, u32[]{:S(2)}) collective-permute-start(bf16[384,768]{1,0:T(8,128)(2,1)S(1)} %get-tuple-element.303.refs_5_), channel_id=1, source_target_pairs={{0,4},{1,5},{2,3},{3,2},{4,0},{5,1},{6,7},{7,6},{8,12},{9,13},{10,... | collective-permute-start | bytes 1769480 | tf_op jit(solution)/shard_map/ppermute | solution.py:680
  86.5 29.8 %collective-permute-start.14 = (bf16[768,768]{1,0:T(8,128)(2,1)S(1)}, bf16[768,768]{1,0:T(8,128)(2,1)S(1)}, u32[]{:S(2)}, u32[]{:S(2)}) collective-permute-start(bf16[768,768]{1,0:T(8,128)(2,1)S(1)} %get-tuple-element.188.refs_7_.refs_10_), channel_id=1, source_target_pairs={{0,2},{1,3},{2,0},{3,1},{4,6},{5,7},{6,4},{7,5},{8,10},{9,11},{10,... | collective-permute-start | bytes 3538952 | tf_op jit(solution)/shard_map/ppermute | solution.py:680
  87.4 28.9 %collective-permute-start.13 = (bf16[768,768]{1,0:T(8,128)(2,1)S(1)}, bf16[768,768]{1,0:T(8,128)(2,1)S(1)}, u32[]{:S(2)}, u32[]{:S(2)}) collective-permute-start(bf16[768,768]{1,0:T(8,128)(2,1)S(1)} %add_convert_fusion.1.refs_6_.refs_9_), channel_id=1, source_target_pairs={{0,1},{1,0},{2,6},{3,7},{4,5},{5,4},{6,2},{7,3},{8,9},{9,8},{10,14... | collective-permute-start | bytes 3538952 | tf_op jit(solution)/shard_map/ppermute | solution.py:680
  99.6 16.7 %collective-permute-start.10 = (bf16[96,768]{1,0:T(8,128)(2,1)S(1)}, bf16[96,768]{1,0:T(8,128)(2,1)S(1)}, u32[]{:S(2)}, u32[]{:S(2)}) collective-permute-start(bf16[96,768]{1,0:T(8,128)(2,1)S(1)} %get-tuple-element.317.refs_6_), channel_id=1, source_target_pairs={{0,16},{1,17},{2,18},{3,19},{4,20},{5,21},{6,22},{7,23},{8,24},{9,... | collective-permute-start | bytes 442376 | tf_op jit(solution)/shard_map/ppermute | solution.py:680
  102.3 14.1 %collective-permute-start.11 = (bf16[96,768]{1,0:T(8,128)(2,1)S(1)}, bf16[96,768]{1,0:T(8,128)(2,1)S(1)}, u32[]{:S(2)}, u32[]{:S(2)}) collective-permute-start(bf16[96,768]{1,0:T(8,128)(2,1)S(1)} %get-tuple-element.316.refs_7_), channel_id=1, source_target_pairs={{0,8},{1,9},{2,10},{3,11},{4,12},{5,13},{6,14},{7,15},{8,0},{9,1},... | collective-permute-start | bytes 442376 | tf_op jit(solution)/shard_map/ppermute | solution.py:680
  103.8 12.5 %collective-permute-start.12 = (bf16[96,768]{1,0:T(8,128)(2,1)S(1)}, bf16[96,768]{1,0:T(8,128)(2,1)S(1)}, u32[]{:S(2)}, u32[]{:S(2)}) collective-permute-start(bf16[96,768]{1,0:T(8,128)(2,1)S(1)} %get-tuple-element.315.refs_8_), channel_id=1, source_target_pairs={{0,24},{1,25},{2,26},{3,27},{4,28},{5,29},{6,30},{7,31},{8,16},{9,... | collective-permute-start | bytes 442376 | tf_op jit(solution)/shard_map/ppermute | solution.py:680
  116.4 4.1 %collective-permute-start.15 = (bf16[768,768]{1,0:T(8,128)(2,1)S(1)}, bf16[768,768]{1,0:T(8,128)(2,1)S(1)}, u32[]{:S(2)}, u32[]{:S(2)}) collective-permute-start(bf16[768,768]{1,0:T(8,128)(2,1)S(1)} %get-tuple-element.206), channel_id=1, source_target_pairs={{0,2},{1,3},{2,0},{3,1},{4,6},{5,7},{6,4},{7,5},{8,10},{9,11},{10,... | collective-permute-start | bytes 3538952 | tf_op jit(solution)/shard_map/ppermute | solution.py:680
  117.0 17.3 %collective-permute-start.18 = (bf16[384,768]{1,0:T(8,128)(2,1)S(1)}, bf16[384,768]{1,0:T(8,128)(2,1)S(1)}, u32[]{:S(2)}, u32[]{:S(2)}) collective-permute-start(bf16[384,768]{1,0:T(8,128)(2,1)S(1)} %get-tuple-element.299.refs_12_), channel_id=1, source_target_pairs={{0,4},{1,5},{2,3},{3,2},{4,0},{5,1},{6,7},{7,6},{8,12},{9,13},{10,... | collective-permute-start | bytes 1769480 | tf_op jit(solution)/shard_map/ppermute | solution.py:680
  118.7 15.6 %collective-permute-start.17 = (bf16[96,768]{1,0:T(8,128)(2,1)S(1)}, bf16[96,768]{1,0:T(8,128)(2,1)S(1)}, u32[]{:S(2)}, u32[]{:S(2)}) collective-permute-start(bf16[96,768]{1,0:T(8,128)(2,1)S(1)} %add_convert_fusion.23.refs_11_), channel_id=1, source_target_pairs={{0,16},{1,17},{2,18},{3,19},{4,20},{5,21},{6,22},{7,23},{8,24},{9,... | collective-permute-start | bytes 442376 | tf_op jit(solution)/shard_map/ppermute | solution.py:680
  120.8 13.6 %collective-permute-start.16 = (bf16[384,768]{1,0:T(8,128)(2,1)S(1)}, bf16[384,768]{1,0:T(8,128)(2,1)S(1)}, u32[]{:S(2)}, u32[]{:S(2)}) collective-permute-start(bf16[384,768]{1,0:T(8,128)(2,1)S(1)} %get-tuple-element.301.refs_10_), channel_id=1, source_target_pairs={{0,1},{1,0},{2,6},{3,7},{4,5},{5,4},{6,2},{7,3},{8,9},{9,8},{10,14... | collective-permute-start | bytes 1769480 | tf_op jit(solution)/shard_map/ppermute | solution.py:680
  134.4 6.5 %collective-permute-start.19 = (bf16[768,768]{1,0:T(8,128)(2,1)S(1)}, bf16[768,768]{1,0:T(8,128)(2,1)S(1)}, u32[]{:S(2)}, u32[]{:S(2)}) collective-permute-start(bf16[768,768]{1,0:T(8,128)(2,1)S(1)} %get-tuple-element.223), channel_id=1, source_target_pairs={{0,2},{1,3},{2,0},{3,1},{4,6},{5,7},{6,4},{7,5},{8,10},{9,11},{10,... | collective-permute-start | bytes 3538952 | tf_op jit(solution)/shard_map/ppermute | solution.py:680
  134.6 10.8 %collective-permute-start.23 = (bf16[96,768]{1,0:T(8,128)(2,1)S(1)}, bf16[96,768]{1,0:T(8,128)(2,1)S(1)}, u32[]{:S(2)}, u32[]{:S(2)}) collective-permute-start(bf16[96,768]{1,0:T(8,128)(2,1)S(1)} %get-tuple-element.314.refs_11_), channel_id=1, source_target_pairs={{0,16},{1,17},{2,18},{3,19},{4,20},{5,21},{6,22},{7,23},{8,24},{9,... | collective-permute-start | bytes 442376 | tf_op jit(solution)/shard_map/ppermute | solution.py:680
  135.9 19.5 %collective-permute-start.24 = (bf16[96,768]{1,0:T(8,128)(2,1)S(1)}, bf16[96,768]{1,0:T(8,128)(2,1)S(1)}, u32[]{:S(2)}, u32[]{:S(2)}) collective-permute-start(bf16[96,768]{1,0:T(8,128)(2,1)S(1)} %get-tuple-element.313.refs_12_), channel_id=1, source_target_pairs={{0,8},{1,9},{2,10},{3,11},{4,12},{5,13},{6,14},{7,15},{8,0},{9,1},... | collective-permute-start | bytes 442376 | tf_op jit(solution)/shard_map/ppermute | solution.py:680
  138.1 17.3 %collective-permute-start.25 = (bf16[96,768]{1,0:T(8,128)(2,1)S(1)}, bf16[96,768]{1,0:T(8,128)(2,1)S(1)}, u32[]{:S(2)}, u32[]{:S(2)}) collective-permute-start(bf16[96,768]{1,0:T(8,128)(2,1)S(1)} %get-tuple-element.312.refs_13_), channel_id=1, source_target_pairs={{0,24},{1,25},{2,26},{3,27},{4,28},{5,29},{6,30},{7,31},{8,16},{9,... | collective-permute-start | bytes 442376 | tf_op jit(solution)/shard_map/ppermute | solution.py:680
  139.5 15.9 %collective-permute-start.22 = (bf16[192,768]{1,0:T(8,128)(2,1)S(1)}, bf16[192,768]{1,0:T(8,128)(2,1)S(1)}, u32[]{:S(2)}, u32[]{:S(2)}) collective-permute-start(bf16[192,768]{1,0:T(8,128)(2,1)S(1)} %pad_maximum_fusion.5.refs_10_), channel_id=1, source_target_pairs={{0,8},{1,9},{2,10},{3,11},{4,12},{5,13},{6,14},{7,15},{8,0},{9,1},... | collective-permute-start | bytes 884744 | tf_op jit(solution)/shard_map/ppermute | solution.py:680
  140.9 14.5 %collective-permute-start.20 = (bf16[192,768]{1,0:T(8,128)(2,1)S(1)}, bf16[192,768]{1,0:T(8,128)(2,1)S(1)}, u32[]{:S(2)}, u32[]{:S(2)}) collective-permute-start(bf16[192,768]{1,0:T(8,128)(2,1)S(1)} %get-tuple-element.311.refs_8_), channel_id=1, source_target_pairs={{0,4},{1,5},{2,3},{3,2},{4,0},{5,1},{6,7},{7,6},{8,12},{9,13},{10,... | collective-permute-start | bytes 884744 | tf_op jit(solution)/shard_map/ppermute | solution.py:680
  145.4 10.1 %collective-permute-start.21 = (bf16[384,768]{1,0:T(8,128)(2,1)S(1)}, bf16[384,768]{1,0:T(8,128)(2,1)S(1)}, u32[]{:S(2)}, u32[]{:S(2)}) collective-permute-start(bf16[384,768]{1,0:T(8,128)(2,1)S(1)} %get-tuple-element.297.refs_9_), channel_id=1, source_target_pairs={{0,1},{1,0},{2,6},{3,7},{4,5},{5,4},{6,2},{7,3},{8,9},{9,8},{10,14... | collective-permute-start | bytes 1769480 | tf_op jit(solution)/shard_map/ppermute | solution.py:680
  155.5 17.6 %collective-permute-start.28 = (bf16[384,768]{1,0:T(8,128)(2,1)S(1)}, bf16[384,768]{1,0:T(8,128)(2,1)S(1)}, u32[]{:S(2)}, u32[]{:S(2)}) collective-permute-start(bf16[384,768]{1,0:T(8,128)(2,1)S(1)} %pad_maximum_fusion.2.refs_8_.refs_9_.refs_1_), channel_id=1, source_target_pairs={{0,4},{1,5},{2,6},{3,7},{4,0},{5,1},{6,2},{7,3},{8,12},{9,13},{10,... | collective-permute-start | bytes 1769480 | tf_op jit(solution)/shard_map/ppermute | solution.py:680
  156.3 16.7 %collective-permute-start.29 = (bf16[384,768]{1,0:T(8,128)(2,1)S(1)}, bf16[384,768]{1,0:T(8,128)(2,1)S(1)}, u32[]{:S(2)}, u32[]{:S(2)}) collective-permute-start(bf16[384,768]{1,0:T(8,128)(2,1)S(1)} %pad_maximum_fusion.2.refs_8_.refs_9_.refs_1_), channel_id=1, source_target_pairs={{0,2},{1,3},{2,0},{3,1},{4,6},{5,7},{6,4},{7,5},{8,10},{9,11},{10,... | collective-permute-start | bytes 1769480 | tf_op jit(solution)/shard_map/ppermute | solution.py:680
  156.4 13.1 %collective-permute-start.30 = (bf16[96,768]{1,0:T(8,128)(2,1)S(1)}, bf16[96,768]{1,0:T(8,128)(2,1)S(1)}, u32[]{:S(2)}, u32[]{:S(2)}) collective-permute-start(bf16[96,768]{1,0:T(8,128)(2,1)S(1)} %add_convert_fusion.17.refs_10_), channel_id=1, source_target_pairs={{0,16},{1,17},{2,18},{3,19},{4,20},{5,21},{6,22},{7,23},{8,24},{9,... | collective-permute-start | bytes 442376 | tf_op jit(solution)/shard_map/ppermute | solution.py:680
  158.3 11.2 %collective-permute-start.27 = (bf16[96,768]{1,0:T(8,128)(2,1)S(1)}, bf16[96,768]{1,0:T(8,128)(2,1)S(1)}, u32[]{:S(2)}, u32[]{:S(2)}) collective-permute-start(bf16[96,768]{1,0:T(8,128)(2,1)S(1)} %get-tuple-element.319.refs_7_), channel_id=1, source_target_pairs={{0,8},{1,9},{2,10},{3,11},{4,12},{5,13},{6,14},{7,15},{8,0},{9,1},... | collective-permute-start | bytes 442376 | tf_op jit(solution)/shard_map/ppermute | solution.py:680
  160.1 12.9 %collective-permute-start.26 = (bf16[192,768]{1,0:T(8,128)(2,1)S(1)}, bf16[192,768]{1,0:T(8,128)(2,1)S(1)}, u32[]{:S(2)}, u32[]{:S(2)}) collective-permute-start(bf16[192,768]{1,0:T(8,128)(2,1)S(1)} %get-tuple-element.309.refs_6_), channel_id=1, source_target_pairs={{0,4},{1,5},{2,3},{3,2},{4,0},{5,1},{6,7},{7,6},{8,12},{9,13},{10,... | collective-permute-start | bytes 884744 | tf_op jit(solution)/shard_map/ppermute | solution.py:680
  173.1 5.0 %collective-permute-start.37 = (f32[8448]{0:T(1024)S(1)}, f32[8448]{0:T(1024)S(1)}, u32[]{:S(2)}, u32[]{:S(2)}) collective-permute-start(f32[8448]{0:T(1024)S(1)} %pad_maximum_fusion.9), channel_id=1, source_target_pairs={{0,1},{1,0},{2,3},{3,2},{4,5},{5,4},{6,7},{7,6},{8,9},{9,8},{10,11... | collective-permute-start | bytes 101384 | tf_op jit(solution)/shard_map/ppermute | solution.py:680
  174.3 17.6 %collective-permute-start.35 = (bf16[384,768]{1,0:T(8,128)(2,1)S(1)}, bf16[384,768]{1,0:T(8,128)(2,1)S(1)}, u32[]{:S(2)}, u32[]{:S(2)}) collective-permute-start(bf16[384,768]{1,0:T(8,128)(2,1)S(1)} %collective-permute-done.28.refs_2_), channel_id=1, source_target_pairs={{0,2},{1,3},{2,0},{3,1},{4,6},{5,7},{6,4},{7,5},{8,10},{9,11},{10,... | collective-permute-start | bytes 1769480 | tf_op jit(solution)/shard_map/ppermute | solution.py:680
  174.3 17.6 %collective-permute-start.36 = (bf16[192,768]{1,0:T(8,128)(2,1)S(1)}, bf16[192,768]{1,0:T(8,128)(2,1)S(1)}, u32[]{:S(2)}, u32[]{:S(2)}) collective-permute-start(bf16[192,768]{1,0:T(8,128)(2,1)S(1)} %pad_maximum_fusion.6), channel_id=1, source_target_pairs={{0,8},{1,9},{2,10},{3,11},{4,12},{5,13},{6,14},{7,15},{8,0},{9,1},... | collective-permute-start | bytes 884744 | tf_op jit(solution)/shard_map/ppermute | solution.py:680
  174.9 8.9 %collective-permute-start.34 = (bf16[48,768]{1,0:T(8,128)(2,1)S(1)}, bf16[48,768]{1,0:T(8,128)(2,1)S(1)}, u32[]{:S(2)}, u32[]{:S(2)}) collective-permute-start(bf16[48,768]{1,0:T(8,128)(2,1)S(1)} %add_convert_fusion.32), channel_id=1, source_target_pairs={{0,16},{1,17},{2,18},{3,19},{4,20},{5,21},{6,22},{7,23},{8,24},{9,... | collective-permute-start | bytes 221192 | tf_op jit(solution)/shard_map/ppermute | solution.py:680
  178.0 9.0 %collective-permute-start.31 = (bf16[48,768]{1,0:T(8,128)(2,1)S(1)}, bf16[48,768]{1,0:T(8,128)(2,1)S(1)}, u32[]{:S(2)}, u32[]{:S(2)}) collective-permute-start(bf16[48,768]{1,0:T(8,128)(2,1)S(1)} %get-tuple-element.322), channel_id=1, source_target_pairs={{0,16},{1,17},{2,18},{3,19},{4,20},{5,21},{6,22},{7,23},{8,24},{9,... | collective-permute-start | bytes 221192 | tf_op jit(solution)/shard_map/ppermute | solution.py:680
  178.1 10.4 %collective-permute-start.32 = (bf16[48,768]{1,0:T(8,128)(2,1)S(1)}, bf16[48,768]{1,0:T(8,128)(2,1)S(1)}, u32[]{:S(2)}, u32[]{:S(2)}) collective-permute-start(bf16[48,768]{1,0:T(8,128)(2,1)S(1)} %get-tuple-element.321), channel_id=1, source_target_pairs={{0,8},{1,9},{2,10},{3,11},{4,12},{5,13},{6,14},{7,15},{8,0},{9,1},... | collective-permute-start | bytes 221192 | tf_op jit(solution)/shard_map/ppermute | solution.py:680
  183.7 8.1 %collective-permute-start.33 = (bf16[48,768]{1,0:T(8,128)(2,1)S(1)}, bf16[48,768]{1,0:T(8,128)(2,1)S(1)}, u32[]{:S(2)}, u32[]{:S(2)}) collective-permute-start(bf16[48,768]{1,0:T(8,128)(2,1)S(1)} %get-tuple-element.320), channel_id=1, source_target_pairs={{0,24},{1,25},{2,26},{3,27},{4,28},{5,29},{6,30},{7,31},{8,16},{9,... | collective-permute-start | bytes 221192 | tf_op jit(solution)/shard_map/ppermute | solution.py:680
  191.9 15.2 %collective-permute-start.41 = (bf16[384,768]{1,0:T(8,128)(2,1)S(1)}, bf16[384,768]{1,0:T(8,128)(2,1)S(1)}, u32[]{:S(2)}, u32[]{:S(2)}) collective-permute-start(bf16[384,768]{1,0:T(8,128)(2,1)S(1)} %pad_maximum_fusion.3.refs_8_.refs_9_.refs_1_), channel_id=1, source_target_pairs={{0,4},{1,5},{2,6},{3,7},{4,0},{5,1},{6,2},{7,3},{8,12},{9,13},{10,... | collective-permute-start | bytes 1769480 | tf_op jit(solution)/shard_map/ppermute | solution.py:680
  192.5 14.7 %collective-permute-start.42 = (bf16[384,768]{1,0:T(8,128)(2,1)S(1)}, bf16[384,768]{1,0:T(8,128)(2,1)S(1)}, u32[]{:S(2)}, u32[]{:S(2)}) collective-permute-start(bf16[384,768]{1,0:T(8,128)(2,1)S(1)} %pad_maximum_fusion.3.refs_8_.refs_9_.refs_1_), channel_id=1, source_target_pairs={{0,2},{1,3},{2,0},{3,1},{4,6},{5,7},{6,4},{7,5},{8,10},{9,11},{10,... | collective-permute-start | bytes 1769480 | tf_op jit(solution)/shard_map/ppermute | solution.py:680
  193.2 11.6 %collective-permute-start.38 = (bf16[48,1536]{1,0:T(8,128)(2,1)S(1)}, bf16[48,1536]{1,0:T(8,128)(2,1)S(1)}, u32[]{:S(2)}, u32[]{:S(2)}) collective-permute-start(bf16[48,1536]{1,0:T(8,128)(2,1)S(1)} %get-tuple-element.324.refs_5_.refs_6_.refs_7_), channel_id=1, source_target_pairs={{0,16},{1,17},{2,18},{3,19},{4,20},{5,21},{6,22},{7,23},{8,24},{9,... | collective-permute-start | bytes 442376 | tf_op jit(solution)/shard_map/ppermute | solution.py:680
  194.2 10.6 %collective-permute-start.39 = (bf16[48,1536]{1,0:T(8,128)(2,1)S(1)}, bf16[48,1536]{1,0:T(8,128)(2,1)S(1)}, u32[]{:S(2)}, u32[]{:S(2)}) collective-permute-start(bf16[48,1536]{1,0:T(8,128)(2,1)S(1)} %get-tuple-element.324.refs_5_.refs_6_.refs_7_), channel_id=1, source_target_pairs={{0,8},{1,9},{2,10},{3,11},{4,12},{5,13},{6,14},{7,15},{8,0},{9,1},... | collective-permute-start | bytes 442376 | tf_op jit(solution)/shard_map/ppermute | solution.py:680
  195.3 11.9 %collective-permute-start.40 = (bf16[48,1536]{1,0:T(8,128)(2,1)S(1)}, bf16[48,1536]{1,0:T(8,128)(2,1)S(1)}, u32[]{:S(2)}, u32[]{:S(2)}) collective-permute-start(bf16[48,1536]{1,0:T(8,128)(2,1)S(1)} %get-tuple-element.324.refs_5_.refs_6_.refs_7_), channel_id=1, source_target_pairs={{0,24},{1,25},{2,26},{3,27},{4,28},{5,29},{6,30},{7,31},{8,16},{9,... | collective-permute-start | bytes 442376 | tf_op jit(solution)/shard_map/ppermute | solution.py:680
  207.2 4.0 %collective-permute-start.46 = (f32[8448]{0:T(1024)S(1)}, f32[8448]{0:T(1024)S(1)}, u32[]{:S(2)}, u32[]{:S(2)}) collective-permute-start(f32[8448]{0:T(1024)S(1)} %fusion), channel_id=1, source_target_pairs={{0,4},{1,5},{2,6},{3,7},{4,0},{5,1},{6,2},{7,3},{8,12},{9,13},{10,... | collective-permute-start | bytes 101384 | tf_op jit(solution)/shard_map/ppermute | solution.py:680
  208.8 9.9 %collective-permute-start.44 = (bf16[192,1536]{1,0:T(8,128)(2,1)S(1)}, bf16[192,1536]{1,0:T(8,128)(2,1)S(1)}, u32[]{:S(2)}, u32[]{:S(2)}) collective-permute-start(bf16[192,1536]{1,0:T(8,128)(2,1)S(1)} %pad_maximum_fusion.4), channel_id=1, source_target_pairs={{0,4},{1,5},{2,3},{3,2},{4,0},{5,1},{6,7},{7,6},{8,12},{9,13},{10,... | collective-permute-start | bytes 1769480 | tf_op jit(solution)/shard_map/ppermute | solution.py:680
  209.4 9.4 %collective-permute-start.45 = (bf16[384,768]{1,0:T(8,128)(2,1)S(1)}, bf16[384,768]{1,0:T(8,128)(2,1)S(1)}, u32[]{:S(2)}, u32[]{:S(2)}) collective-permute-start(bf16[384,768]{1,0:T(8,128)(2,1)S(1)} %collective-permute-done.41.refs_2_), channel_id=1, source_target_pairs={{0,2},{1,3},{2,0},{3,1},{4,6},{5,7},{6,4},{7,5},{8,10},{9,11},{10,... | collective-permute-start | bytes 1769480 | tf_op jit(solution)/shard_map/ppermute | solution.py:680
  218.8 16.3 %collective-permute-start.47 = (bf16[384,1536]{1,0:T(8,128)(2,1)S(1)}, bf16[384,1536]{1,0:T(8,128)(2,1)S(1)}, u32[]{:S(2)}, u32[]{:S(2)}) collective-permute-start(bf16[384,1536]{1,0:T(8,128)(2,1)S(1)} %constant_dynamic-update-slice_fusion.refs_7_.refs_8_.refs_1_), channel_id=1, source_target_pairs={{0,1},{1,0},{2,6},{3,7},{4,5},{5,4},{6,2},{7,3},{8,9},{9,8},{10,14... | collective-permute-start | bytes 3538952 | tf_op jit(solution)/shard_map/ppermute | solution.py:680
  219.7 15.3 %collective-permute-start.48 = (bf16[384,1536]{1,0:T(8,128)(2,1)S(1)}, bf16[384,1536]{1,0:T(8,128)(2,1)S(1)}, u32[]{:S(2)}, u32[]{:S(2)}) collective-permute-start(bf16[384,1536]{1,0:T(8,128)(2,1)S(1)} %constant_dynamic-update-slice_fusion.refs_7_.refs_8_.refs_1_), channel_id=1, source_target_pairs={{0,2},{1,3},{2,0},{3,1},{4,6},{5,7},{6,4},{7,5},{8,10},{9,11},{10,... | collective-permute-start | bytes 3538952 | tf_op jit(solution)/shard_map/ppermute | solution.py:680
  219.7 9.1 %collective-permute-start.49 = (f32[8448]{0:T(1024)S(1)}, f32[8448]{0:T(1024)S(1)}, u32[]{:S(2)}, u32[]{:S(2)}) collective-permute-start(f32[8448]{0:T(1024)S(1)} %add.278.refs_9_.refs_10_.refs_11_), channel_id=1, source_target_pairs={{0,16},{1,17},{2,18},{3,19},{4,20},{5,21},{6,22},{7,23},{8,24},{9,... | collective-permute-start | bytes 101384 | tf_op jit(solution)/shard_map/ppermute | solution.py:680
  222.6 6.2 %collective-permute-start.50 = (f32[8448]{0:T(1024)S(1)}, f32[8448]{0:T(1024)S(1)}, u32[]{:S(2)}, u32[]{:S(2)}) collective-permute-start(f32[8448]{0:T(1024)S(1)} %add.278.refs_9_.refs_10_.refs_11_), channel_id=1, source_target_pairs={{0,8},{1,9},{2,10},{3,11},{4,12},{5,13},{6,14},{7,15},{8,0},{9,1},... | collective-permute-start | bytes 101384 | tf_op jit(solution)/shard_map/ppermute | solution.py:680
  222.7 6.1 %collective-permute-start.51 = (f32[8448]{0:T(1024)S(1)}, f32[8448]{0:T(1024)S(1)}, u32[]{:S(2)}, u32[]{:S(2)}) collective-permute-start(f32[8448]{0:T(1024)S(1)} %add.278.refs_9_.refs_10_.refs_11_), channel_id=1, source_target_pairs={{0,24},{1,25},{2,26},{3,27},{4,28},{5,29},{6,30},{7,31},{8,16},{9,... | collective-permute-start | bytes 101384 | tf_op jit(solution)/shard_map/ppermute | solution.py:680
  (40 other events, 222.4 us)
